TPU v7x, 128 devices: a whole 4x4x4 slice. The times are simulated.
128 devices in a mesh: factor: 4 (over z), pair: 32 (over x, y, core).
Axes of the slice: x: 4, y: 4, z: 4, core: 2. Of those that a mesh axis runs over, the one named last changes fastest.
Arguments:
- columns: float32 [16384, 4096], P('factor', 'pair'), parts along dimension 0, may hold values from -250 to 250
- basis: float32 [16384, 4096], P('factor', 'pair'), parts along dimension 0, may hold values from -6 to 6
Outputs:
- new_columns: float32 [16384, 4096], P('factor', 'pair'), parts along dimension 0
- new_basis: float32 [16384, 4096], P('factor', 'pair'), parts along dimension 0
There are 4 independent parts, one for each index of `factor`. A program takes and returns all parts, laid end to end along the dimension named above; each array names one. Nothing has to cross between parts.
All inputs are finite; a program needn't handle non-finite values.
Results may differ from a plain program's by a relative error of at most 0.0014.
Values sent between devices are 32-bit elements; how exact they have to be, the bound alone decides.
A program may use at most 128 MiB of HBM per device.

v0:
```python
import functools

import jax
import jax.numpy as jnp
from jax import lax
from jax.experimental import pallas as pl
from jax.experimental.pallas import tpu as pltpu
from jax.sharding import PartitionSpec as P

STEPS = 6
INNER_ROUNDS = 8
MESH = pl.DeviceIdType.MESH
F32 = jnp.float32
BF16 = jnp.bfloat16
WIDTH = 128
HALF = 64
ROWS = 512


def iota(shape, dim):
    return lax.broadcasted_iota(jnp.int32, shape, dim)


def partner_of(place, round_no):
    cycle = WIDTH - 1
    j = round_no % cycle
    mirror = 1 + lax.rem(cycle - 2 + 2 * j + 2 * cycle - (place - 1), cycle)
    lone = 1 + (cycle - 1 + j) % cycle
    return jnp.where(place == 0, lone, jnp.where(place == lone, 0, mirror))


def role_of(place, round_no):
    cycle = WIDTH - 1
    j = round_no % cycle
    position = 1 + lax.rem(place - 1 - j + 2 * cycle, cycle)
    return (place == 0) | (position < HALF)


def pick_lanes(value, index):
    return jnp.take_along_axis(value, index, axis=1)


def rsqrt(value):
    guess = lax.rsqrt(value)
    return guess * (1.5 - 0.5 * value * guess * guess)


def angles(diag, cross, partner, first):
    other = pick_lanes(diag, partner)
    spread = jnp.where(first, diag - other, other - diag)
    flip = jnp.where(spread >= 0.0, 1.0, -1.0)
    size = jnp.abs(spread)
    twice = 2.0 * cross * flip
    most = jnp.maximum(size, jnp.abs(twice))
    still = most == 0.0
    most = jnp.where(still, 1.0, most)
    size = jnp.where(still, 1.0, size / most)
    twice = twice / most
    inverse = rsqrt(size * size + twice * twice)
    cos_sq = 0.5 + 0.5 * size * inverse
    inverse_cos = rsqrt(cos_sq)
    cosine = cos_sq * inverse_cos
    sine = 0.5 * twice * inverse * inverse_cos
    return cosine, jnp.where(first, sine, -sine)


def rotations(gram):
    rows = iota((WIDTH, WIDTH), 0)
    lanes = iota((WIDTH, WIDTH), 1)
    few = iota((8, WIDTH), 1)
    current = gram
    accumulated = jnp.where(rows == lanes, 1.0, 0.0).astype(F32)
    for round_no in range(INNER_ROUNDS):
        partner = partner_of(lanes, round_no)
        diag = jnp.sum(jnp.where(rows == lanes, current, 0.0), axis=0, keepdims=True)
        cross = jnp.sum(jnp.where(rows == partner, current, 0.0), axis=0, keepdims=True)
        diag = jnp.broadcast_to(diag, (8, WIDTH))
        cross = jnp.broadcast_to(cross, (8, WIDTH))
        cosine, sine = angles(
            diag, cross, partner_of(few, round_no), role_of(few, round_no)
        )
        cosine = jnp.broadcast_to(cosine[:1], (WIDTH, WIDTH))
        sine = jnp.broadcast_to(sine[:1], (WIDTH, WIDTH))
        turn = lambda m: m * cosine + pick_lanes(m, partner) * sine
        accumulated = turn(accumulated)
        if round_no + 1 < INNER_ROUNDS:
            current = turn(turn(current).T)
    return accumulated


def swap_halves(value):
    return pltpu.roll(value, HALF, 1)


def split(value, parts):
    out = []
    for _ in range(parts - 1):
        part = value.astype(BF16)
        out.append(part)
        value = value - part.astype(F32)
    out.append(value.astype(BF16))
    return out


def folded(big):
    low = iota((HALF, WIDTH), 1) < HALF
    halves = []
    for at in (0, WIDTH):
        one, two = big[at:at + HALF], big[at + HALF:at + WIDTH]
        left = one[:, :WIDTH] + swap_halves(two[:, :WIDTH])
        right = swap_halves(one[:, WIDTH:]) + two[:, WIDTH:]
        halves.append(jnp.where(low, left, right))
    return jnp.concatenate(halves, axis=0)


def expanded(turn, is_first):
    low = iota((HALF, WIDTH), 1) < HALF
    out = []
    for at in (0, HALF):
        rows = turn[at:at + HALF]
        moved = swap_halves(rows)
        for keep in (low, ~low):
            to_upper = jnp.where(keep, rows if keep is low else moved, 0.0)
            to_lower = jnp.where(keep, moved if keep is low else rows, 0.0)
            one = jnp.where(is_first, to_lower, to_upper)
            two = jnp.where(is_first, to_upper, to_lower)
            out.append(jnp.concatenate([one, two], axis=1))
    return jnp.concatenate(out, axis=0)


def kernel(
    slots, x_in, v_in, x_out, v_out,
    panels, staged, gram_sum, turn_parts, load_sem, store_sem, send_sem, recv_sem,
):
    packed = panels.shape[2]
    me = lax.axis_index("pair")
    factor = lax.axis_index("factor")
    right = lax.rem(me + 1, slots)
    left = lax.rem(me + slots - 1, slots)
    is_first = 1 - (me + slots - 1) // slots
    is_last = (me + 1) // slots

    loads = []
    for which, source in enumerate((x_in, v_in)):
        load = pltpu.make_async_copy(source, staged.at[which], load_sem.at[which])
        load.start()
        loads.append(load)

    barrier = pltpu.get_barrier_semaphore()
    for neighbour in (left, right):
        pl.semaphore_signal(
            barrier, inc=1, device_id=(factor, neighbour), device_id_type=MESH
        )
    pl.semaphore_wait(barrier, 2)

    def place(step, side):
        return 2 * step + side

    def rows_of(chunk):
        return pl.ds(pl.multiple_of(chunk * ROWS, ROWS), ROWS)

    def remote(which, step, chunk, side, device):
        return pltpu.make_async_remote_copy(
            src_ref=panels.at[which, place(step, side), rows_of(chunk)],
            dst_ref=panels.at[which, place(step + 1, side), rows_of(chunk)],
            send_sem=send_sem.at[which, place(step, side), chunk],
            recv_sem=recv_sem.at[which, place(step, side), chunk],
            device_id=(factor, device),
            device_id_type=MESH,
        )

    def to_right(which, step, chunk):
        return remote(which, step, chunk, 0, right)

    def to_left(which, step, chunk):
        return remote(which, step, chunk, 1, left)

    def send(which, step, chunk):
        @pl.when(me < slots - 1)
        def _():
            to_right(which, step, chunk).start()

        @pl.when(me > 0)
        def _():
            to_left(which, step, chunk).start()

    def wait_sent(which, step, chunk):
        @pl.when(me < slots - 1)
        def _():
            to_right(which, step, chunk).wait_send()

        @pl.when(me > 0)
        def _():
            to_left(which, step, chunk).wait_send()

    def wait_received(which, step, chunk):
        @pl.when(me > 0)
        def _():
            to_right(which, step, chunk).wait_recv()

        @pl.when(me < slots - 1)
        def _():
            to_left(which, step, chunk).wait_recv()

    def every_chunk(act):
        def body(chunk, _):
            act(chunk)
            return 0

        lax.fori_loop(0, packed // ROWS, body, 0)

    def pack(which):
        low = iota((ROWS, WIDTH), 1) < HALF

        def body(chunk, _):
            at = pl.ds(pl.multiple_of(chunk * ROWS, ROWS), ROWS)
            other = pl.ds(
                pl.multiple_of(packed + chunk * ROWS, ROWS), ROWS
            )
            one, two = staged[which, at], staged[which, other]
            panels[which, 0, at] = jnp.where(low, one, swap_halves(two))
            panels[which, 1, at] = jnp.where(low, swap_halves(one), two)
            return 0

        lax.fori_loop(0, packed // ROWS, body, 0)

    def unpack(which):
        low = iota((ROWS, WIDTH), 1) < HALF

        def body(chunk, _):
            at = pl.ds(pl.multiple_of(chunk * ROWS, ROWS), ROWS)
            other = pl.ds(
                pl.multiple_of(packed + chunk * ROWS, ROWS), ROWS
            )
            upper = panels[which, place(STEPS, 0), at]
            lower = panels[which, place(STEPS, 1), at]
            staged[which, at] = jnp.where(low, upper, swap_halves(lower))
            staged[which, other] = jnp.where(low, swap_halves(upper), lower)
            return 0

        lax.fori_loop(0, packed // ROWS, body, 0)

    def panel_rows(which, step, at):
        return jnp.concatenate(
            [panels[which, place(step, 0), at], panels[which, place(step, 1), at]], axis=1
        )

    def gram(step):
        gram_sum[...] = jnp.zeros_like(gram_sum)
        inner = lambda a, b: lax.dot_general(
            a, b, (((0,), (0,)), ((), ())), preferred_element_type=F32
        )

        def add(chunk):
            @pl.when(step > 0)
            def _():
                wait_received(0, step - 1, chunk)

            high, low = split(panel_rows(0, step, rows_of(chunk)), 2)
            gram_sum[0] += inner(high, high) + inner(low, low)
            gram_sum[1] += inner(high, low)

        every_chunk(add)
        mixed = gram_sum[1]
        return folded(gram_sum[0] + (mixed + mixed.T))

    def apply(which, step, chunk, terms):
        at = rows_of(chunk)
        high, low = split(panel_rows(which, step, at), 2)
        total = jnp.dot(high, turn_parts[0], preferred_element_type=F32)
        small = jnp.dot(low, turn_parts[0], preferred_element_type=F32)
        for term in range(1, terms):
            small += jnp.dot(high, turn_parts[term], preferred_element_type=F32)
        total += small
        panels[which, place(step, 0) + 3 * is_last, at] = total[:, :WIDTH]
        panels[which, place(step, 1) + is_first, at] = total[:, WIDTH:]

    loads[0].wait()
    pack(0)

    def one_step(step, _):
        sums = gram(step)

        @pl.when(step > 0)
        def _():
            every_chunk(lambda chunk: send(1, step - 1, chunk))

        turn = rotations(sums)
        for term, part in enumerate(split(expanded(turn, is_first == 1), 3)):
            turn_parts[term] = part

        def turn_columns(chunk):
            apply(0, step, chunk, 3)
            send(0, step, chunk)

        every_chunk(turn_columns)

        @pl.when(step == 0)
        def _():
            loads[1].wait()
            pack(1)

        def turn_basis(chunk):
            @pl.when(step > 0)
            def _():
                wait_received(1, step - 1, chunk)

            apply(1, step, chunk, 2)

        every_chunk(turn_basis)
        return 0

    lax.fori_loop(0, STEPS, one_step, 0)
    every_chunk(lambda chunk: wait_received(0, STEPS - 1, chunk))
    every_chunk(lambda chunk: send(1, STEPS - 1, chunk))

    stores = []
    for which, target in enumerate((x_out, v_out)):
        if which:
            every_chunk(lambda chunk: wait_received(1, STEPS - 1, chunk))
        unpack(which)
        store = pltpu.make_async_copy(staged.at[which], target, store_sem.at[which])
        store.start()
        stores.append(store)

    def settle(step, _):
        for which in range(2):
            every_chunk(lambda chunk: wait_sent(which, step, chunk))
        return 0

    lax.fori_loop(0, STEPS, settle, 0)
    for store in stores:
        store.wait()


def on_device(columns, basis):
    rows, width = columns.shape
    slots = lax.axis_size("pair")
    packed = rows // 2
    shape = jax.ShapeDtypeStruct((rows, width), F32)
    return pl.pallas_call(
        functools.partial(kernel, slots),
        out_shape=(shape, shape),
        in_specs=[pl.BlockSpec(memory_space=pl.ANY)] * 2,
        out_specs=(pl.BlockSpec(memory_space=pl.ANY),) * 2,
        scratch_shapes=[
            pltpu.VMEM((2, 2 * STEPS + 2, packed, width), F32),
            pltpu.VMEM((2, rows, width), F32),
            pltpu.VMEM((2, 2 * width, 2 * width), F32),
            pltpu.VMEM((3, 2 * width, 2 * width), BF16),
            pltpu.SemaphoreType.DMA((2,)),
            pltpu.SemaphoreType.DMA((2,)),
            pltpu.SemaphoreType.DMA((2, 2 * STEPS, packed // ROWS)),
            pltpu.SemaphoreType.DMA((2, 2 * STEPS, packed // ROWS)),
        ],
        compiler_params=pltpu.CompilerParams(
            collective_id=0, has_side_effects=True, vmem_limit_bytes=50 * 2**20
        ),
        cost_estimate=pl.CostEstimate(
            flops=6 * 9 * 2 * rows * width * width,
            bytes_accessed=4 * rows * width * 4,
            transcendentals=0,
        ),
    )(columns, basis)


def solution(mesh):
    spec = P("factor", "pair")
    return jax.shard_map(
        on_device, mesh=mesh, in_specs=(spec, spec), out_specs=(spec, spec), check_vma=False
    )
```

profile of v0, /device:TPU:102, one launch (start us, length us, event | category | flops | bytes accessed | tf_op | source)
XLA Modules:
  0.0 176.2 jit_solution(16120916589788858442)
XLA Ops:
  0.6 171.9 %shard_map.41 = (f32[4096,128]{1,0:T(8,128)S(1)}, f32[4096,128]{1,0:T(8,128)}) custom-call(f32[4096,128]{1,0:T(8,128)} %x_in.1, f32[4096,128]{1,0:T(8,128)} %v_in.1), custom_call_target="tpu_custom_call" | custom-call | flops 7247757312 | bytes 8388608 | tf_op jit(solution)/shard_map/pallas_call | solution.py:341
  172.6 0.0 copy-start
  172.6 1.3 copy.6
  173.9 1.0 copy-done
  174.9 1.3 copy.7
Async XLA Ops:
  172.6 2.3 %copy-start = (f32[4096,128]{1,0:T(8,128)S(1)}, f32[4096,128]{1,0:T(8,128)}, u32[]{:S(2)}) copy-start(f32[4096,128]{1,0:T(8,128)} %get-tuple-element.5) | copy-start | bytes 6291460
where the time goes:
time: 176 us
  Pallas kernels  172 us (98%)
  local copies, waits for them, and re-layouts  3.66 us (2%)
    pallas_call x1, Pallas kernels, on_device(): pl.pallas_call(functools.partial(kernel, slots), out_shape=(shape, shape)...  172 us
    unnamed x4, local copies, waits for them, and re-layouts  3.66 us

commit v1 on v0

v1 whole, which is shorter than its diff:
```python
import functools

import jax
import jax.numpy as jnp
from jax import lax
from jax.experimental import pallas as pl
from jax.experimental.pallas import tpu as pltpu
from jax.sharding import PartitionSpec as P

STEPS = 6
INNER_ROUNDS = 8
MESH = pl.DeviceIdType.MESH
F32 = jnp.float32
BF16 = jnp.bfloat16
WIDTH = 128
HALF = 64
GRAM_ROWS = 512
APPLY_ROWS = 512


def iota(shape, dim):
    return lax.broadcasted_iota(jnp.int32, shape, dim)


def rsqrt(value):
    guess = lax.rsqrt(value)
    return guess * (1.5 - 0.5 * value * guess * guess)


def sublane_roll(value, shift):
    return pltpu.roll(value, shift % 8, 0)


def order_of(row, shift):
    inside = lax.rem(row, HALF)
    k = 8 * lax.rem(inside, 8) + inside // 8
    k = jnp.where(row < HALF, k, WIDTH - 1 - k)
    return jnp.where(k == 0, 0, 1 + lax.rem(k - 1 + shift, WIDTH - 1))


def order_matrix(shift):
    rows = iota((WIDTH, WIDTH), 0)
    lanes = iota((WIDTH, WIDTH), 1)
    return jnp.where(order_of(rows, shift) == lanes, 1.0, 0.0).astype(F32)


def moved_on(first, second):
    top = iota((8, first.shape[1]), 0) == 0
    end = iota((8, first.shape[1]), 0) == 7
    a, b = first, second
    new_first = jnp.concatenate(
        [
            jnp.where(top, a[:8], a[8:16]),
            a[16:],
            jnp.where(end, b[HALF - 8:], sublane_roll(a[:8], -1)),
        ],
        axis=0,
    )
    new_second = jnp.concatenate(
        [jnp.where(top, a[8:16], sublane_roll(b[HALF - 8:], 1)), b[:HALF - 8]], axis=0
    )
    return new_first, new_second


def angles(diag_a, diag_b, cross):
    spread = diag_a - diag_b
    twice = 2.0 * cross
    twice = jnp.where(spread >= 0.0, twice, -twice)
    size = jnp.abs(spread)
    most = jnp.maximum(size, jnp.abs(twice))
    still = most == 0.0
    scale = pl.reciprocal(jnp.where(still, 1.0, most), approx=True)
    size = jnp.where(still, 1.0, size * scale)
    twice = twice * scale
    inverse = rsqrt(size * size + twice * twice)
    cos_sq = 0.5 + 0.5 * size * inverse
    inverse_cos = rsqrt(cos_sq)
    return cos_sq * inverse_cos, 0.5 * twice * inverse * inverse_cos


def lane_sum(value):
    return jnp.broadcast_to(jnp.sum(value, axis=1, keepdims=True), value.shape)


def rotations(gram):
    start = order_matrix(0)
    start_bf16 = start.astype(BF16)
    pieces = [jnp.dot(start_bf16, part, preferred_element_type=F32) for part in split(gram, 3)]
    ordered = (pieces[0] + pieces[1]) + pieces[2]
    turn_a, turn_b = start[:HALF], start[HALF:]
    with_a, with_b = ordered[:HALF], ordered[HALF:]
    diag_a, diag_b = lane_sum(turn_a * with_a), lane_sum(turn_b * with_b)
    for round_no in range(INNER_ROUNDS):
        cross = lane_sum(turn_a * with_b)
        cosine, sine = angles(diag_a, diag_b, cross)
        turn_a, turn_b = cosine * turn_a + sine * turn_b, cosine * turn_b - sine * turn_a
        if round_no + 1 < INNER_ROUNDS:
            with_a, with_b = cosine * with_a + sine * with_b, cosine * with_b - sine * with_a
            both = 2.0 * cosine * sine * cross
            cos_sq, sin_sq = cosine * cosine, sine * sine
            diag_a, diag_b = (
                cos_sq * diag_a + sin_sq * diag_b + both,
                cos_sq * diag_b + sin_sq * diag_a - both,
            )
            turn_a, turn_b = moved_on(turn_a, turn_b)
            with_a, with_b = moved_on(with_a, with_b)
            diag_a, diag_b = moved_on(diag_a, diag_b)
    end = order_matrix(INNER_ROUNDS - 1).astype(BF16)
    turn = jnp.concatenate([turn_a, turn_b], axis=0)
    pieces = [
        lax.dot_general(part, end, (((0,), (0,)), ((), ())), preferred_element_type=F32)
        for part in split(turn, 3)
    ]
    return (pieces[0] + pieces[1]) + pieces[2]


def swap_halves(value):
    return pltpu.roll(value, HALF, 1)


def split(value, parts):
    out = []
    for _ in range(parts - 1):
        part = value.astype(BF16)
        out.append(part)
        value = value - part.astype(F32)
    out.append(value.astype(BF16))
    return out


def folded(big):
    low = iota((HALF, WIDTH), 1) < HALF
    halves = []
    for at in (0, WIDTH):
        one, two = big[at:at + HALF], big[at + HALF:at + WIDTH]
        left = one[:, :WIDTH] + swap_halves(two[:, :WIDTH])
        right = swap_halves(one[:, WIDTH:]) + two[:, WIDTH:]
        halves.append(jnp.where(low, left, right))
    return jnp.concatenate(halves, axis=0)


def expanded(turn, is_first):
    low = iota((HALF, WIDTH), 1) < HALF
    out = []
    for at in (0, HALF):
        rows = turn[at:at + HALF]
        moved = swap_halves(rows)
        for keep in (low, ~low):
            to_upper = jnp.where(keep, rows if keep is low else moved, 0.0)
            to_lower = jnp.where(keep, moved if keep is low else rows, 0.0)
            one = jnp.where(is_first, to_lower, to_upper)
            two = jnp.where(is_first, to_upper, to_lower)
            out.append(jnp.concatenate([one, two], axis=1))
    return jnp.concatenate(out, axis=0)


def kernel(
    slots, x_in, v_in, x_out, v_out,
    panels, staged, gram_sum, turn_parts, load_sem, store_sem, send_sem, recv_sem,
):
    packed = panels.shape[2]
    me = lax.axis_index("pair")
    factor = lax.axis_index("factor")
    right = lax.rem(me + 1, slots)
    left = lax.rem(me + slots - 1, slots)
    is_first = 1 - (me + slots - 1) // slots
    is_last = (me + 1) // slots

    loads = []
    for which, source in enumerate((x_in, v_in)):
        load = pltpu.make_async_copy(source, staged.at[which], load_sem.at[which])
        load.start()
        loads.append(load)

    barrier = pltpu.get_barrier_semaphore()
    for neighbour in (left, right):
        pl.semaphore_signal(
            barrier, inc=1, device_id=(factor, neighbour), device_id_type=MESH
        )
    pl.semaphore_wait(barrier, 2)

    def place(step, side):
        return 2 * step + side

    def to_right(which, step):
        return pltpu.make_async_remote_copy(
            src_ref=panels.at[which, place(step, 0)],
            dst_ref=panels.at[which, place(step + 1, 0)],
            send_sem=send_sem.at[which, place(step, 0)],
            recv_sem=recv_sem.at[which, place(step, 0)],
            device_id=(factor, right),
            device_id_type=MESH,
        )

    def to_left(which, step):
        return pltpu.make_async_remote_copy(
            src_ref=panels.at[which, place(step, 1)],
            dst_ref=panels.at[which, place(step + 1, 1)],
            send_sem=send_sem.at[which, place(step, 1)],
            recv_sem=recv_sem.at[which, place(step, 1)],
            device_id=(factor, left),
            device_id_type=MESH,
        )

    def send(which, step):
        @pl.when(me < slots - 1)
        def _():
            to_right(which, step).start()

        @pl.when(me > 0)
        def _():
            to_left(which, step).start()

    def wait_sent(which, step):
        @pl.when(me < slots - 1)
        def _():
            to_right(which, step).wait_send()

        @pl.when(me > 0)
        def _():
            to_left(which, step).wait_send()

    def wait_received(which, step):
        @pl.when(me > 0)
        def _():
            to_right(which, step).wait_recv()

        @pl.when(me < slots - 1)
        def _():
            to_left(which, step).wait_recv()

    def pack(which):
        low = iota((APPLY_ROWS, WIDTH), 1) < HALF

        def body(chunk, _):
            at = pl.ds(pl.multiple_of(chunk * APPLY_ROWS, APPLY_ROWS), APPLY_ROWS)
            other = pl.ds(
                pl.multiple_of(packed + chunk * APPLY_ROWS, APPLY_ROWS), APPLY_ROWS
            )
            one, two = staged[which, at], staged[which, other]
            panels[which, 0, at] = jnp.where(low, one, swap_halves(two))
            panels[which, 1, at] = jnp.where(low, swap_halves(one), two)
            return 0

        lax.fori_loop(0, packed // APPLY_ROWS, body, 0)

    def unpack(which):
        low = iota((APPLY_ROWS, WIDTH), 1) < HALF

        def body(chunk, _):
            at = pl.ds(pl.multiple_of(chunk * APPLY_ROWS, APPLY_ROWS), APPLY_ROWS)
            other = pl.ds(
                pl.multiple_of(packed + chunk * APPLY_ROWS, APPLY_ROWS), APPLY_ROWS
            )
            upper = panels[which, place(STEPS, 0), at]
            lower = panels[which, place(STEPS, 1), at]
            staged[which, at] = jnp.where(low, upper, swap_halves(lower))
            staged[which, other] = jnp.where(low, swap_halves(upper), lower)
            return 0

        lax.fori_loop(0, packed // APPLY_ROWS, body, 0)

    def panel_rows(which, step, at):
        return jnp.concatenate(
            [panels[which, place(step, 0), at], panels[which, place(step, 1), at]], axis=1
        )

    def gram(step):
        gram_sum[...] = jnp.zeros_like(gram_sum)
        inner = lambda a, b: lax.dot_general(
            a, b, (((0,), (0,)), ((), ())), preferred_element_type=F32
        )

        def body(chunk, _):
            at = pl.ds(pl.multiple_of(chunk * GRAM_ROWS, GRAM_ROWS), GRAM_ROWS)
            high, low = split(panel_rows(0, step, at), 2)
            gram_sum[0] += inner(high, high) + inner(low, low)
            gram_sum[1] += inner(high, low)
            return 0

        lax.fori_loop(0, packed // GRAM_ROWS, body, 0)
        mixed = gram_sum[1]
        return folded(gram_sum[0] + (mixed + mixed.T))

    def apply(which, step, terms):
        first_place = place(step, 0) + 3 * is_last
        second_place = place(step, 1) + is_first

        def body(chunk, _):
            at = pl.ds(pl.multiple_of(chunk * APPLY_ROWS, APPLY_ROWS), APPLY_ROWS)
            high, low = split(panel_rows(which, step, at), 2)
            total = jnp.dot(high, turn_parts[0], preferred_element_type=F32)
            small = jnp.dot(low, turn_parts[0], preferred_element_type=F32)
            for term in range(1, terms):
                small += jnp.dot(high, turn_parts[term], preferred_element_type=F32)
            total += small
            panels[which, first_place, at] = total[:, :WIDTH]
            panels[which, second_place, at] = total[:, WIDTH:]
            return 0

        lax.fori_loop(0, packed // APPLY_ROWS, body, 0)

    loads[0].wait()
    pack(0)

    def one_step(step, _):
        @pl.when(step > 0)
        def _():
            wait_received(0, step - 1)

        turn = rotations(gram(step))
        for term, part in enumerate(split(expanded(turn, is_first == 1), 3)):
            turn_parts[term] = part
        apply(0, step, 3)
        send(0, step)

        @pl.when(step == 0)
        def _():
            loads[1].wait()
            pack(1)

        @pl.when(step > 0)
        def _():
            wait_received(1, step - 1)

        apply(1, step, 2)
        send(1, step)
        return 0

    lax.fori_loop(0, STEPS, one_step, 0)

    stores = []
    for which, target in enumerate((x_out, v_out)):
        wait_received(which, STEPS - 1)
        unpack(which)
        store = pltpu.make_async_copy(staged.at[which], target, store_sem.at[which])
        store.start()
        stores.append(store)

    def settle(step, _):
        for which in range(2):
            wait_sent(which, step)
        return 0

    lax.fori_loop(0, STEPS, settle, 0)
    for store in stores:
        store.wait()


def on_device(columns, basis):
    rows, width = columns.shape
    slots = lax.axis_size("pair")
    packed = rows // 2
    shape = jax.ShapeDtypeStruct((rows, width), F32)
    return pl.pallas_call(
        functools.partial(kernel, slots),
        out_shape=(shape, shape),
        in_specs=[pl.BlockSpec(memory_space=pl.ANY)] * 2,
        out_specs=(pl.BlockSpec(memory_space=pl.ANY),) * 2,
        scratch_shapes=[
            pltpu.VMEM((2, 2 * STEPS + 2, packed, width), F32),
            pltpu.VMEM((2, rows, width), F32),
            pltpu.VMEM((2, 2 * width, 2 * width), F32),
            pltpu.VMEM((3, 2 * width, 2 * width), BF16),
            pltpu.SemaphoreType.DMA((2,)),
            pltpu.SemaphoreType.DMA((2,)),
            pltpu.SemaphoreType.DMA((2, 2 * STEPS)),
            pltpu.SemaphoreType.DMA((2, 2 * STEPS)),
        ],
        compiler_params=pltpu.CompilerParams(
            collective_id=0, has_side_effects=True, vmem_limit_bytes=50 * 2**20
        ),
        cost_estimate=pl.CostEstimate(
            flops=6 * 9 * 2 * rows * width * width,
            bytes_accessed=4 * rows * width * 4,
            transcendentals=0,
        ),
    )(columns, basis)


def solution(mesh):
    spec = P("factor", "pair")
    return jax.shard_map(
        on_device, mesh=mesh, in_specs=(spec, spec), out_specs=(spec, spec), check_vma=False
    )
```

time: 176 us -> 154 us (0.88)
  the two profiles are of different devices: /device:TPU:102 before, /device:TPU:1 now
where the time goes in v1:
time: 154 us; the launch traced here: 153 us
  Pallas kernels  149 us (97%)
  local copies, waits for them, and re-layouts  3.66 us (2%)
    pallas_call x1, Pallas kernels, on_device(): pl.pallas_call(functools.partial(kernel, slots), out_shape=(shape, shape)...  149 us
    unnamed x4, local copies, waits for them, and re-layouts  3.66 us

profile of v1, /device:TPU:1, one launch (start us, length us, event | category | flops | bytes accessed | tf_op | source)
XLA Modules:
  0.0 153.4 jit_solution(1620895882001917099)
XLA Ops:
  0.6 149.1 %shard_map.41 = (f32[4096,128]{1,0:T(8,128)S(1)}, f32[4096,128]{1,0:T(8,128)}) custom-call(f32[4096,128]{1,0:T(8,128)} %x_in.1, f32[4096,128]{1,0:T(8,128)} %v_in.1), custom_call_target="tpu_custom_call" | custom-call | flops 7247757312 | bytes 8388608 | tf_op jit(solution)/shard_map/pallas_call | solution.py:355
  149.8 0.0 copy-start
  149.8 1.3 copy.6
  151.1 1.0 copy-done
  152.1 1.3 copy.7
Async XLA Ops:
  149.8 2.3 %copy-start = (f32[4096,128]{1,0:T(8,128)S(1)}, f32[4096,128]{1,0:T(8,128)}, u32[]{:S(2)}) copy-start(f32[4096,128]{1,0:T(8,128)} %get-tuple-element.5) | copy-start | bytes 6291460

commit v2 on v0

--- a/solution.py
+++ b/solution.py
@@ -21,71 +21,96 @@
     return lax.broadcasted_iota(jnp.int32, shape, dim)
 
 
-def partner_of(place, round_no):
-    cycle = WIDTH - 1
-    j = round_no % cycle
-    mirror = 1 + lax.rem(cycle - 2 + 2 * j + 2 * cycle - (place - 1), cycle)
-    lone = 1 + (cycle - 1 + j) % cycle
-    return jnp.where(place == 0, lone, jnp.where(place == lone, 0, mirror))
-
-
-def role_of(place, round_no):
-    cycle = WIDTH - 1
-    j = round_no % cycle
-    position = 1 + lax.rem(place - 1 - j + 2 * cycle, cycle)
-    return (place == 0) | (position < HALF)
-
-
-def pick_lanes(value, index):
-    return jnp.take_along_axis(value, index, axis=1)
-
-
 def rsqrt(value):
     guess = lax.rsqrt(value)
     return guess * (1.5 - 0.5 * value * guess * guess)
 
 
-def angles(diag, cross, partner, first):
-    other = pick_lanes(diag, partner)
-    spread = jnp.where(first, diag - other, other - diag)
-    flip = jnp.where(spread >= 0.0, 1.0, -1.0)
+def sublane_roll(value, shift):
+    return pltpu.roll(value, shift % 8, 0)
+
+
+def order_of(row, shift):
+    inside = lax.rem(row, HALF)
+    k = 8 * lax.rem(inside, 8) + inside // 8
+    k = jnp.where(row < HALF, k, WIDTH - 1 - k)
+    return jnp.where(k == 0, 0, 1 + lax.rem(k - 1 + shift, WIDTH - 1))
+
+
+def order_matrix(shift):
+    rows = iota((WIDTH, WIDTH), 0)
+    lanes = iota((WIDTH, WIDTH), 1)
+    return jnp.where(order_of(rows, shift) == lanes, 1.0, 0.0).astype(F32)
+
+
+def moved_on(first, second):
+    top = iota((8, first.shape[1]), 0) == 0
+    end = iota((8, first.shape[1]), 0) == 7
+    a, b = first, second
+    new_first = jnp.concatenate(
+        [
+            jnp.where(top, a[:8], a[8:16]),
+            a[16:],
+            jnp.where(end, b[HALF - 8:], sublane_roll(a[:8], -1)),
+        ],
+        axis=0,
+    )
+    new_second = jnp.concatenate(
+        [jnp.where(top, a[8:16], sublane_roll(b[HALF - 8:], 1)), b[:HALF - 8]], axis=0
+    )
+    return new_first, new_second
+
+
+def angles(diag_a, diag_b, cross):
+    spread = diag_a - diag_b
+    twice = 2.0 * cross
+    twice = jnp.where(spread >= 0.0, twice, -twice)
     size = jnp.abs(spread)
-    twice = 2.0 * cross * flip
     most = jnp.maximum(size, jnp.abs(twice))
     still = most == 0.0
-    most = jnp.where(still, 1.0, most)
-    size = jnp.where(still, 1.0, size / most)
-    twice = twice / most
+    scale = pl.reciprocal(jnp.where(still, 1.0, most), approx=True)
+    size = jnp.where(still, 1.0, size * scale)
+    twice = twice * scale
     inverse = rsqrt(size * size + twice * twice)
     cos_sq = 0.5 + 0.5 * size * inverse
     inverse_cos = rsqrt(cos_sq)
-    cosine = cos_sq * inverse_cos
-    sine = 0.5 * twice * inverse * inverse_cos
-    return cosine, jnp.where(first, sine, -sine)
+    return cos_sq * inverse_cos, 0.5 * twice * inverse * inverse_cos
+
+
+def lane_sum(value):
+    return jnp.broadcast_to(jnp.sum(value, axis=1, keepdims=True), value.shape)
 
 
 def rotations(gram):
-    rows = iota((WIDTH, WIDTH), 0)
-    lanes = iota((WIDTH, WIDTH), 1)
-    few = iota((8, WIDTH), 1)
-    current = gram
-    accumulated = jnp.where(rows == lanes, 1.0, 0.0).astype(F32)
+    start = order_matrix(0)
+    start_bf16 = start.astype(BF16)
+    pieces = [jnp.dot(start_bf16, part, preferred_element_type=F32) for part in split(gram, 3)]
+    ordered = (pieces[0] + pieces[1]) + pieces[2]
+    turn_a, turn_b = start[:HALF], start[HALF:]
+    with_a, with_b = ordered[:HALF], ordered[HALF:]
+    diag_a, diag_b = lane_sum(turn_a * with_a), lane_sum(turn_b * with_b)
     for round_no in range(INNER_ROUNDS):
-        partner = partner_of(lanes, round_no)
-        diag = jnp.sum(jnp.where(rows == lanes, current, 0.0), axis=0, keepdims=True)
-        cross = jnp.sum(jnp.where(rows == partner, current, 0.0), axis=0, keepdims=True)
-        diag = jnp.broadcast_to(diag, (8, WIDTH))
-        cross = jnp.broadcast_to(cross, (8, WIDTH))
-        cosine, sine = angles(
-            diag, cross, partner_of(few, round_no), role_of(few, round_no)
-        )
-        cosine = jnp.broadcast_to(cosine[:1], (WIDTH, WIDTH))
-        sine = jnp.broadcast_to(sine[:1], (WIDTH, WIDTH))
-        turn = lambda m: m * cosine + pick_lanes(m, partner) * sine
-        accumulated = turn(accumulated)
+        cross = lane_sum(turn_a * with_b)
+        cosine, sine = angles(diag_a, diag_b, cross)
+        turn_a, turn_b = cosine * turn_a + sine * turn_b, cosine * turn_b - sine * turn_a
         if round_no + 1 < INNER_ROUNDS:
-            current = turn(turn(current).T)
-    return accumulated
+            with_a, with_b = cosine * with_a + sine * with_b, cosine * with_b - sine * with_a
+            both = 2.0 * cosine * sine * cross
+            cos_sq, sin_sq = cosine * cosine, sine * sine
+            diag_a, diag_b = (
+                cos_sq * diag_a + sin_sq * diag_b + both,
+                cos_sq * diag_b + sin_sq * diag_a - both,
+            )
+            turn_a, turn_b = moved_on(turn_a, turn_b)
+            with_a, with_b = moved_on(with_a, with_b)
+            diag_a, diag_b = moved_on(diag_a, diag_b)
+    end = order_matrix(INNER_ROUNDS - 1).astype(BF16)
+    turn = jnp.concatenate([turn_a, turn_b], axis=0)
+    pieces = [
+        lax.dot_general(part, end, (((0,), (0,)), ((), ())), preferred_element_type=F32)
+        for part in split(turn, 3)
+    ]
+    return (pieces[0] + pieces[1]) + pieces[2]
 
 
 def swap_halves(value):
@@ -281,10 +306,6 @@
     def one_step(step, _):
         sums = gram(step)
 
-        @pl.when(step > 0)
-        def _():
-            every_chunk(lambda chunk: send(1, step - 1, chunk))
-
         turn = rotations(sums)
         for term, part in enumerate(split(expanded(turn, is_first == 1), 3)):
             turn_parts[term] = part
@@ -306,13 +327,13 @@
                 wait_received(1, step - 1, chunk)
 
             apply(1, step, chunk, 2)
+            send(1, step, chunk)
 
         every_chunk(turn_basis)
         return 0
 
     lax.fori_loop(0, STEPS, one_step, 0)
     every_chunk(lambda chunk: wait_received(0, STEPS - 1, chunk))
-    every_chunk(lambda chunk: send(1, STEPS - 1, chunk))
 
     stores = []
     for which, target in enumerate((x_out, v_out)):

time: 176 us -> 154 us (0.88)
  the two profiles are of different devices: /device:TPU:102 before, /device:TPU:1 now
where the time goes in v2:
time: 154 us; the launch traced here: 153 us
  Pallas kernels  149 us (97%)
  local copies, waits for them, and re-layouts  3.66 us (2%)
    pallas_call x1, Pallas kernels, on_device(): pl.pallas_call(functools.partial(kernel, slots), out_shape=(shape, shape)...  149 us
    unnamed x4, local copies, waits for them, and re-layouts  3.66 us

profile of v2, /device:TPU:1, one launch (start us, length us, event | category | flops | bytes accessed | tf_op | source)
XLA Modules:
  0.0 153.4 jit_solution(17094370944387365920)
XLA Ops:
  0.6 149.0 %shard_map.41 = (f32[4096,128]{1,0:T(8,128)S(1)}, f32[4096,128]{1,0:T(8,128)}) custom-call(f32[4096,128]{1,0:T(8,128)} %x_in.1, f32[4096,128]{1,0:T(8,128)} %v_in.1), custom_call_target="tpu_custom_call" | custom-call | flops 7247757312 | bytes 8388608 | tf_op jit(solution)/shard_map/pallas_call | solution.py:362
  149.7 0.0 copy-start
  149.7 1.3 copy.6
  151.0 1.0 copy-done
  152.0 1.3 copy.7
Async XLA Ops:
  149.7 2.3 %copy-start = (f32[4096,128]{1,0:T(8,128)S(1)}, f32[4096,128]{1,0:T(8,128)}, u32[]{:S(2)}) copy-start(f32[4096,128]{1,0:T(8,128)} %get-tuple-element.5) | copy-start | bytes 6291460

commit v3 on v2

v3 whole, which is shorter than its diff:
```python
import functools

import jax
import jax.numpy as jnp
from jax import lax
from jax.experimental import pallas as pl
from jax.experimental.pallas import tpu as pltpu
from jax.sharding import PartitionSpec as P

STEPS = 6
INNER_ROUNDS = 8
MESH = pl.DeviceIdType.MESH
F32 = jnp.float32
BF16 = jnp.bfloat16
WIDTH = 128
HALF = 64
ROWS = 512
RING = 8


def iota(shape, dim):
    return lax.broadcasted_iota(jnp.int32, shape, dim)


def rsqrt(value):
    guess = lax.rsqrt(value)
    return guess * (1.5 - 0.5 * value * guess * guess)


def sublane_roll(value, shift):
    return pltpu.roll(value, shift % 8, 0)


def order_of(row, shift):
    inside = lax.rem(row, HALF)
    k = 8 * lax.rem(inside, 8) + inside // 8
    k = jnp.where(row < HALF, k, WIDTH - 1 - k)
    return jnp.where(k == 0, 0, 1 + lax.rem(k - 1 + shift, WIDTH - 1))


def order_matrix(shift):
    rows = iota((WIDTH, WIDTH), 0)
    lanes = iota((WIDTH, WIDTH), 1)
    return jnp.where(order_of(rows, shift) == lanes, 1.0, 0.0).astype(F32)


def moved_on(first, second):
    top = iota((8, first.shape[1]), 0) == 0
    end = iota((8, first.shape[1]), 0) == 7
    a, b = first, second
    new_first = jnp.concatenate(
        [
            jnp.where(top, a[:8], a[8:16]),
            a[16:],
            jnp.where(end, b[HALF - 8:], sublane_roll(a[:8], -1)),
        ],
        axis=0,
    )
    new_second = jnp.concatenate(
        [jnp.where(top, a[8:16], sublane_roll(b[HALF - 8:], 1)), b[:HALF - 8]], axis=0
    )
    return new_first, new_second


def angles(diag_a, diag_b, cross):
    spread = diag_a - diag_b
    twice = 2.0 * cross
    twice = jnp.where(spread >= 0.0, twice, -twice)
    size = jnp.abs(spread)
    most = jnp.maximum(size, jnp.abs(twice))
    still = most == 0.0
    scale = pl.reciprocal(jnp.where(still, 1.0, most), approx=True)
    size = jnp.where(still, 1.0, size * scale)
    twice = twice * scale
    inverse = rsqrt(size * size + twice * twice)
    cos_sq = 0.5 + 0.5 * size * inverse
    inverse_cos = rsqrt(cos_sq)
    return cos_sq * inverse_cos, 0.5 * twice * inverse * inverse_cos


def lane_sum(value):
    return jnp.broadcast_to(jnp.sum(value, axis=1, keepdims=True), value.shape)


def rotations(gram):
    start = order_matrix(0)
    start_bf16 = start.astype(BF16)
    pieces = [jnp.dot(start_bf16, part, preferred_element_type=F32) for part in split(gram, 3)]
    ordered = (pieces[0] + pieces[1]) + pieces[2]
    turn_a, turn_b = start[:HALF], start[HALF:]
    with_a, with_b = ordered[:HALF], ordered[HALF:]
    diag_a, diag_b = lane_sum(turn_a * with_a), lane_sum(turn_b * with_b)
    lanes = iota((HALF, WIDTH), 1)
    waves = jnp.zeros((HALF, WIDTH), F32)
    for round_no in range(INNER_ROUNDS):
        cross = lane_sum(turn_a * with_b)
        cosine, sine = angles(diag_a, diag_b, cross)
        waves = jnp.where(lanes == round_no, cosine, waves)
        waves = jnp.where(lanes == INNER_ROUNDS + round_no, sine, waves)
        turn_a, turn_b = cosine * turn_a + sine * turn_b, cosine * turn_b - sine * turn_a
        if round_no + 1 < INNER_ROUNDS:
            with_a, with_b = cosine * with_a + sine * with_b, cosine * with_b - sine * with_a
            both = 2.0 * cosine * sine * cross
            cos_sq, sin_sq = cosine * cosine, sine * sine
            diag_a, diag_b = (
                cos_sq * diag_a + sin_sq * diag_b + both,
                cos_sq * diag_b + sin_sq * diag_a - both,
            )
            turn_a, turn_b = moved_on(turn_a, turn_b)
            with_a, with_b = moved_on(with_a, with_b)
            diag_a, diag_b = moved_on(diag_a, diag_b)
    pieces = in_order(turn_a, turn_b, 3)
    return (pieces[0] + pieces[1]) + pieces[2], waves


def in_order(turn_a, turn_b, parts):
    end = order_matrix(INNER_ROUNDS - 1).astype(BF16)
    turn = jnp.concatenate([turn_a, turn_b], axis=0)
    return [
        lax.dot_general(part, end, (((0,), (0,)), ((), ())), preferred_element_type=F32)
        for part in split(turn, parts)
    ]


def multiplied_out(waves):
    columns = jnp.concatenate([waves] * (WIDTH // 16), axis=0).T
    start = order_matrix(0)
    turn_a, turn_b = start[:HALF], start[HALF:]
    for round_no in range(INNER_ROUNDS):
        wide = lambda at: jnp.broadcast_to(columns[:HALF, at:at + 1], (HALF, WIDTH))
        cosine, sine = wide(round_no), wide(INNER_ROUNDS + round_no)
        turn_a, turn_b = cosine * turn_a + sine * turn_b, cosine * turn_b - sine * turn_a
        if round_no + 1 < INNER_ROUNDS:
            turn_a, turn_b = moved_on(turn_a, turn_b)
    return in_order(turn_a, turn_b, 2)


def swap_halves(value):
    return pltpu.roll(value, HALF, 1)


def split(value, parts):
    out = []
    for _ in range(parts - 1):
        part = value.astype(BF16)
        out.append(part)
        value = value - part.astype(F32)
    out.append(value.astype(BF16))
    return out


def folded(big):
    low = iota((HALF, WIDTH), 1) < HALF
    halves = []
    for at in (0, WIDTH):
        one, two = big[at:at + HALF], big[at + HALF:at + WIDTH]
        left = one[:, :WIDTH] + swap_halves(two[:, :WIDTH])
        right = swap_halves(one[:, WIDTH:]) + two[:, WIDTH:]
        halves.append(jnp.where(low, left, right))
    return jnp.concatenate(halves, axis=0)


def expanded(turn, is_first):
    low = iota((HALF, WIDTH), 1) < HALF
    out = []
    for at in (0, HALF):
        rows = turn[at:at + HALF]
        moved = swap_halves(rows)
        for keep in (low, ~low):
            to_upper = jnp.where(keep, rows if keep is low else moved, 0.0)
            to_lower = jnp.where(keep, moved if keep is low else rows, 0.0)
            one = jnp.where(is_first, to_lower, to_upper)
            two = jnp.where(is_first, to_upper, to_lower)
            out.append(jnp.concatenate([one, two], axis=1))
    return jnp.concatenate(out, axis=0)


def loop(low, high, act):
    def body(at, _):
        act(at)
        return 0

    lax.fori_loop(low, high, body, 0)


def kernel(
    slots, x_in, v_in, x_out, v_out,
    panels, staged, gram_sum, turn_parts, held, moving, edge_out, edge_in, waves, weights,
    load_sem, store_sem, send_sem, recv_sem, out_send, in_recv,
    edge_send, edge_recv, wave_send, wave_recv, passing, hop_send, hop_recv, pass_send,
):
    packed = panels.shape[1]
    share = held.shape[1]
    bend = share // 2
    chunks = packed // ROWS
    me = lax.axis_index("pair")
    factor = lax.axis_index("factor")
    right = lax.rem(me + 1, slots)
    left = lax.rem(me + slots - 1, slots)
    is_first = 1 - (me + slots - 1) // slots
    is_last = (me + 1) // slots
    own = lax.rem(me, RING)
    base = me - own
    twin = own + 1 - 2 * lax.rem(own, 2)
    ring_right = lax.rem(me + RING, slots)
    ring_left = lax.rem(me + slots - RING, slots)
    first_ring = me < RING
    last_ring = me >= slots - RING

    def other(offset):
        return lax.rem(own + offset, RING)

    def remote(src, dst, send, recv, device):
        return pltpu.make_async_remote_copy(
            src_ref=src, dst_ref=dst, send_sem=send, recv_sem=recv,
            device_id=(factor, device), device_id_type=MESH,
        )

    def rows_of(chunk, size=ROWS):
        return pl.ds(pl.multiple_of(chunk * size, size), size)

    def place(step, side):
        return 2 * step + side

    def block(step, chunk, side, device):
        at = place(step, side)
        return remote(
            panels.at[at, rows_of(chunk)], panels.at[at + 2, rows_of(chunk)],
            send_sem.at[at, chunk], recv_sem.at[at, chunk], device,
        )

    def send_block(step, chunk):
        @pl.when(me < slots - 1)
        def _():
            block(step, chunk, 0, right).start()

        @pl.when(me > 0)
        def _():
            block(step, chunk, 1, left).start()

    def wait_sent(step, chunk):
        @pl.when(me < slots - 1)
        def _():
            block(step, chunk, 0, right).wait_send()

        @pl.when(me > 0)
        def _():
            block(step, chunk, 1, left).wait_send()

    def wait_received(step, chunk):
        @pl.when(me > 0)
        def _():
            block(step, chunk, 0, right).wait_recv()

        @pl.when(me < slots - 1)
        def _():
            block(step, chunk, 1, left).wait_recv()

    above, below = other(2), other(6)
    above_twin, below_twin = lax.rem(twin + 2, RING), lax.rem(twin + 6, RING)
    opposite = (other(4), lax.rem(twin + 4, RING))
    hop_to = (above, below)
    hop_from = (below, above)
    pass_to = (above, below_twin)

    def rows_from(way, peer):
        return held.at[peer] if way else v_in.at[rows_of(peer, share)]

    def rows_at(way, row):
        return v_out.at[rows_of(row, share)] if way else held.at[row]

    def piece(way, peer, lands):
        return remote(
            rows_from(way, peer), rows_at(way, lands),
            out_send.at[way, peer], in_recv.at[way, lands], base + peer,
        )

    def hop(way, side):
        return remote(
            rows_from(way, opposite[side]), passing.at[way, side],
            hop_send.at[way, side], hop_recv.at[way, side], base + hop_to[side],
        )

    def pass_on(way, side):
        return remote(
            passing.at[way, side], rows_at(way, hop_from[side]),
            pass_send.at[way, side], in_recv.at[way, hop_from[side]], base + pass_to[side],
        )

    def send_piece(way, peer):
        piece(way, peer, own).start()

    def forward(way):
        for side in range(2):
            hop(way, side).wait_recv()
            pass_on(way, side).start()

    def wait_pieces(way):
        loop(1, RING, lambda o: piece(way, other(o), other(o)).wait_recv())

    def wait_pieces_sent(way):
        for peer in (above, below, above_twin, below_twin, twin):
            piece(way, peer, own).wait_send()
        for side in range(2):
            hop(way, side).wait_send()
            pass_on(way, side).wait_send()

    def wave(step, peer, lands):
        return remote(
            waves.at[step, lands], waves.at[step, lands],
            wave_send.at[step, peer], wave_recv.at[step, lands], base + peer,
        )

    def edge(step, side, device):
        return remote(
            edge_out.at[step, side], edge_in.at[step, side],
            edge_send.at[step, side], edge_recv.at[step, side], device,
        )

    def to_edges(act_right, act_left):
        pl.when(jnp.logical_not(last_ring))(act_right)
        pl.when(jnp.logical_not(first_ring))(act_left)

    load = pltpu.make_async_copy(x_in, staged, load_sem.at[0])
    load.start()
    keep_in = pltpu.make_async_copy(
        v_in.at[rows_of(own, share)], held.at[own], load_sem.at[1]
    )
    keep_in.start()

    barrier = pltpu.get_barrier_semaphore()
    for offset in range(1, RING):
        pl.semaphore_signal(
            barrier, inc=1, device_id=(factor, base + other(offset)), device_id_type=MESH
        )
    for neighbour in (left, right, ring_left, ring_right):
        pl.semaphore_signal(
            barrier, inc=1, device_id=(factor, neighbour), device_id_type=MESH
        )
    pl.semaphore_wait(barrier, RING + 3)

    for side in range(2):
        hop(0, side).start()
    send_piece(0, twin)

    def pack():
        low = iota((ROWS, WIDTH), 1) < HALF

        def one(chunk):
            upper, lower = staged[rows_of(chunk)], staged[rows_of(chunk + chunks)]
            panels[0, rows_of(chunk)] = jnp.where(low, upper, swap_halves(lower))
            panels[1, rows_of(chunk)] = jnp.where(low, swap_halves(upper), lower)

        loop(0, chunks, one)

    def unpack():
        low = iota((ROWS, WIDTH), 1) < HALF

        def one(chunk):
            upper = panels[place(STEPS, 0), rows_of(chunk)]
            lower = panels[place(STEPS, 1), rows_of(chunk)]
            staged[rows_of(chunk)] = jnp.where(low, upper, swap_halves(lower))
            staged[rows_of(chunk + chunks)] = jnp.where(low, swap_halves(upper), lower)

        loop(0, chunks, one)

    def panel_rows(step, at):
        return jnp.concatenate(
            [panels[place(step, 0), at], panels[place(step, 1), at]], axis=1
        )

    def gram(step):
        gram_sum[...] = jnp.zeros_like(gram_sum)
        inner = lambda a, b: lax.dot_general(
            a, b, (((0,), (0,)), ((), ())), preferred_element_type=F32
        )

        def add(chunk):
            @pl.when(step > 0)
            def _():
                wait_received(step - 1, chunk)

            @pl.when(chunk == chunks - 1)
            def _():
                @pl.when(step == 1)
                def _():
                    send_piece(0, above)
                    send_piece(0, below)

                @pl.when(step == 2)
                def _():
                    forward(0)

                @pl.when(step == 3)
                def _():
                    send_piece(0, above_twin)
                    send_piece(0, below_twin)

            high, low = split(panel_rows(step, rows_of(chunk)), 2)
            gram_sum[0] += inner(high, high) + inner(low, low)
            gram_sum[1] += inner(high, low)

        loop(0, chunks, add)
        mixed = gram_sum[1]
        return folded(gram_sum[0] + (mixed + mixed.T))

    def apply(step, chunk):
        at = rows_of(chunk)
        high, low = split(panel_rows(step, at), 2)
        dot = lambda a, term: jnp.dot(a, turn_parts[term], preferred_element_type=F32)
        total = dot(high, 0) + (dot(low, 0) + dot(high, 1) + dot(high, 2))
        panels[place(step, 0) + 3 * is_last, at] = total[:, :WIDTH]
        panels[place(step, 1) + is_first, at] = total[:, WIDTH:]

    low_lanes = iota((share, WIDTH), 1) < HALF
    low_bend = iota((bend, WIDTH), 1) < HALF

    def spread_held():
        def one(k):
            upper = held[jnp.minimum(k, RING - 1)]
            lower = held[jnp.maximum(k - 2, 0)]
            moving[0, k] = jnp.where(low_lanes, upper, lower)

        loop(0, RING + 2, one)

    def slot_rows(now, slot):
        return jnp.where(low_lanes, moving[now, slot], moving[now, slot + 2])

    def prepare(step):
        def one(slot):
            @pl.when(slot != own)
            def _():
                wave(step, slot, slot).wait_recv()

            high, low = multiplied_out(waves[step, slot])
            first_slot = first_ring & (slot == 0)
            high = jnp.where(first_slot, swap_halves(high), high)
            low = jnp.where(first_slot, swap_halves(low), low)
            weights[step, slot] = jnp.concatenate([high, low], axis=1).astype(BF16)

        loop(0, RING, one)

    def take_edges(step, now):
        def from_left():
            edge(step, 0, ring_right).wait_recv()
            got = edge_in[step, 0]
            moving[now, 0, :bend] = got
            moving[now, 0, bend:] = swap_halves(got)

        def from_right():
            edge(step, 1, ring_left).wait_recv()
            got = edge_in[step, 1]
            moving[now, RING + 1, :bend] = swap_halves(got)
            moving[now, RING + 1, bend:] = got

        pl.when(jnp.logical_not(first_ring))(from_left)
        pl.when(jnp.logical_not(last_ring))(from_right)

    def turn_basis(step):
        now = lax.rem(step, 2)
        later = 1 - now

        def one(slot):
            high, low = split(slot_rows(now, slot), 2)
            weight = weights[step, slot]
            both = jnp.dot(
                jnp.concatenate([high, low], axis=1),
                jnp.concatenate([weight, weight], axis=0),
                preferred_element_type=F32,
            )
            moving[later, slot + 1] = both[:, :WIDTH] + both[:, WIDTH:]

        loop(1, RING - 1, one)
        pl.when(step > 0)(lambda: take_edges(step - 1, now))
        loop(0, 2, lambda side: one(side * (RING - 1)))

        def up():
            give = moving[later, RING]
            edge_out[step, 0] = jnp.where(low_bend, give[:bend], swap_halves(give[bend:]))
            edge(step, 0, ring_right).start()

        def down():
            give = moving[later, 1]
            edge_out[step, 1] = jnp.where(low_bend, swap_halves(give[:bend]), give[bend:])
            edge(step, 1, ring_left).start()

        to_edges(up, down)

        @pl.when(first_ring)
        def _():
            moving[later, 0] = swap_halves(moving[later, 1])

        @pl.when(last_ring)
        def _():
            moving[later, RING + 1] = swap_halves(moving[later, RING])

    load.wait()
    pack()

    def one_step(step):
        turn, own_waves = rotations(gram(step))
        for term, part in enumerate(split(expanded(turn, is_first == 1), 3)):
            turn_parts[term] = part

        def turn_columns(chunk):
            apply(step, chunk)
            send_block(step, chunk)

        loop(0, chunks, turn_columns)
        blank = jnp.zeros((HALF, WIDTH), F32)
        waves[step, own] = jnp.concatenate([own_waves, blank], axis=0).T[:16]
        loop(1, RING, lambda offset: wave(step, other(offset), own).start())

        loop(step - (step + 5) // 6, step + step // 5, prepare)

        @pl.when(step == 3)
        def _():
            keep_in.wait()
            wait_pieces(0)
            spread_held()

        loop((step // 4) * 2 + (step // 5) * 2, (step // 3 + step // 4 + step // 5) * 2, turn_basis)

    loop(0, STEPS, one_step)

    def gather_rows(slot):
        held[slot] = slot_rows(STEPS % 2, slot)

    take_edges(STEPS - 1, STEPS % 2)
    for side in range(2):
        gather_rows(opposite[side])
        hop(1, side).start()
    for peer in (above, below, above_twin, below_twin, twin):
        gather_rows(peer)
        send_piece(1, peer)
    gather_rows(own)
    keep_out = pltpu.make_async_copy(
        held.at[own], v_out.at[rows_of(own, share)], store_sem.at[1]
    )
    keep_out.start()

    loop(0, chunks, lambda chunk: wait_received(STEPS - 1, chunk))
    unpack()
    store = pltpu.make_async_copy(staged, x_out, store_sem.at[0])
    store.start()

    forward(1)

    def settle(step):
        loop(0, chunks, lambda chunk: wait_sent(step, chunk))
        loop(1, RING, lambda o: wave(step, other(o), own).wait_send())
        to_edges(
            lambda: edge(step, 0, ring_right).wait_send(),
            lambda: edge(step, 1, ring_left).wait_send(),
        )

    loop(0, STEPS, settle)
    wait_pieces_sent(0)
    wait_pieces_sent(1)
    wait_pieces(1)
    store.wait()
    keep_out.wait()


def on_device(columns, basis):
    rows, width = columns.shape
    slots = lax.axis_size("pair")
    packed = rows // 2
    share = rows // RING
    shape = jax.ShapeDtypeStruct((rows, width), F32)
    dma = pltpu.SemaphoreType.DMA
    return pl.pallas_call(
        functools.partial(kernel, slots),
        out_shape=(shape, shape),
        in_specs=[pl.BlockSpec(memory_space=pl.ANY)] * 2,
        out_specs=(pl.BlockSpec(memory_space=pl.ANY),) * 2,
        scratch_shapes=[
            pltpu.VMEM((2 * STEPS + 2, packed, width), F32),
            pltpu.VMEM((rows, width), F32),
            pltpu.VMEM((2, 2 * width, 2 * width), F32),
            pltpu.VMEM((3, 2 * width, 2 * width), BF16),
            pltpu.VMEM((RING, share, width), F32),
            pltpu.VMEM((2, RING + 2, share, width), F32),
            pltpu.VMEM((STEPS, 2, share // 2, width), F32),
            pltpu.VMEM((STEPS, 2, share // 2, width), F32),
            pltpu.VMEM((STEPS, RING, 16, width), F32),
            pltpu.VMEM((STEPS, RING, width, 2 * width), BF16),
            dma((2,)),
            dma((2,)),
            dma((2 * STEPS, packed // ROWS)),
            dma((2 * STEPS, packed // ROWS)),
            dma((2, RING)),
            dma((2, RING)),
            dma((STEPS, 2)),
            dma((STEPS, 2)),
            dma((STEPS, RING)),
            dma((STEPS, RING)),
            pltpu.VMEM((2, 2, share, width), F32),
            dma((2, 2)),
            dma((2, 2)),
            dma((2, 2)),
        ],
        compiler_params=pltpu.CompilerParams(
            collective_id=0, has_side_effects=True, vmem_limit_bytes=50 * 2**20
        ),
        cost_estimate=pl.CostEstimate(
            flops=6 * 9 * 2 * rows * width * width,
            bytes_accessed=4 * rows * width * 4,
            transcendentals=0,
        ),
    )(columns, basis)


def solution(mesh):
    spec = P("factor", "pair")
    return jax.shard_map(
        on_device, mesh=mesh, in_specs=(spec, spec), out_specs=(spec, spec), check_vma=False
    )
```

time: 154 us -> 172 us (1.12)
  Pallas kernels: 149 us -> 168 us
    pallas_call x1, Pallas kernels: 149 us -> 168 us  [on_device(): pl.pallas_call(functools.partial(kernel, slots), out_shape=(shape, shape)...]
where the time goes in v3:
time: 172 us
  Pallas kernels  168 us (98%)
  local copies, waits for them, and re-layouts  3.66 us (2%)
    pallas_call x1, Pallas kernels, on_device(): pl.pallas_call(functools.partial(kernel, slots), out_shape=(shape, shape)...  168 us
    unnamed x4, local copies, waits for them, and re-layouts  3.66 us

profile of v3, /device:TPU:1, one launch (start us, length us, event | category | flops | bytes accessed | tf_op | source)
XLA Modules:
  0.0 171.8 jit_solution(7008362479189714093)
XLA Ops:
  0.6 167.5 %shard_map.41 = (f32[4096,128]{1,0:T(8,128)S(1)}, f32[4096,128]{1,0:T(8,128)}) custom-call(f32[4096,128]{1,0:T(8,128)} %x_in.1, f32[4096,128]{1,0:T(8,128)} %v_in.1), custom_call_target="tpu_custom_call" | custom-call | flops 7247757312 | bytes 8388608 | tf_op jit(solution)/shard_map/pallas_call | solution.py:572
  168.2 0.0 copy-start
  168.2 1.3 copy.6
  169.5 1.0 copy-done
  170.5 1.3 copy.7
Async XLA Ops:
  168.2 2.3 %copy-start = (f32[4096,128]{1,0:T(8,128)S(1)}, f32[4096,128]{1,0:T(8,128)}, u32[]{:S(2)}) copy-start(f32[4096,128]{1,0:T(8,128)} %get-tuple-element.5) | copy-start | bytes 6291460

commit v4 on v3

--- a/solution.py
+++ b/solution.py
@@ -14,7 +14,7 @@
 BF16 = jnp.bfloat16
 WIDTH = 128
 HALF = 64
-ROWS = 512
+LONG = 1024
 RING = 8
 
 
@@ -36,12 +36,6 @@
     k = 8 * lax.rem(inside, 8) + inside // 8
     k = jnp.where(row < HALF, k, WIDTH - 1 - k)
     return jnp.where(k == 0, 0, 1 + lax.rem(k - 1 + shift, WIDTH - 1))
-
-
-def order_matrix(shift):
-    rows = iota((WIDTH, WIDTH), 0)
-    lanes = iota((WIDTH, WIDTH), 1)
-    return jnp.where(order_of(rows, shift) == lanes, 1.0, 0.0).astype(F32)
 
 
 def moved_on(first, second):
@@ -82,10 +76,9 @@
     return jnp.broadcast_to(jnp.sum(value, axis=1, keepdims=True), value.shape)
 
 
-def rotations(gram):
-    start = order_matrix(0)
-    start_bf16 = start.astype(BF16)
-    pieces = [jnp.dot(start_bf16, part, preferred_element_type=F32) for part in split(gram, 3)]
+def rotations(gram, start):
+    order = start.astype(BF16)
+    pieces = [jnp.dot(order, part, preferred_element_type=F32) for part in split(gram, 3)]
     ordered = (pieces[0] + pieces[1]) + pieces[2]
     turn_a, turn_b = start[:HALF], start[HALF:]
     with_a, with_b = ordered[:HALF], ordered[HALF:]
@@ -109,30 +102,21 @@
             turn_a, turn_b = moved_on(turn_a, turn_b)
             with_a, with_b = moved_on(with_a, with_b)
             diag_a, diag_b = moved_on(diag_a, diag_b)
-    pieces = in_order(turn_a, turn_b, 3)
-    return (pieces[0] + pieces[1]) + pieces[2], waves
-
-
-def in_order(turn_a, turn_b, parts):
-    end = order_matrix(INNER_ROUNDS - 1).astype(BF16)
-    turn = jnp.concatenate([turn_a, turn_b], axis=0)
+    return jnp.concatenate([turn_a, turn_b], axis=0), waves
+
+
+def final_order(swapped):
+    rows = iota((WIDTH, WIDTH), 0)
+    rows = lax.rem(rows + HALF, WIDTH) if swapped else rows
+    lanes = iota((WIDTH, WIDTH), 1)
+    return jnp.where(order_of(lanes, INNER_ROUNDS - 1) == rows, 1.0, 0.0).astype(BF16)
+
+
+def in_order(turn, order, parts):
     return [
-        lax.dot_general(part, end, (((0,), (0,)), ((), ())), preferred_element_type=F32)
+        jnp.dot(order, part, preferred_element_type=F32).astype(BF16)
         for part in split(turn, parts)
     ]
-
-
-def multiplied_out(waves):
-    columns = jnp.concatenate([waves] * (WIDTH // 16), axis=0).T
-    start = order_matrix(0)
-    turn_a, turn_b = start[:HALF], start[HALF:]
-    for round_no in range(INNER_ROUNDS):
-        wide = lambda at: jnp.broadcast_to(columns[:HALF, at:at + 1], (HALF, WIDTH))
-        cosine, sine = wide(round_no), wide(INNER_ROUNDS + round_no)
-        turn_a, turn_b = cosine * turn_a + sine * turn_b, cosine * turn_b - sine * turn_a
-        if round_no + 1 < INNER_ROUNDS:
-            turn_a, turn_b = moved_on(turn_a, turn_b)
-    return in_order(turn_a, turn_b, 2)
 
 
 def swap_halves(value):
@@ -149,32 +133,6 @@
     return out
 
 
-def folded(big):
-    low = iota((HALF, WIDTH), 1) < HALF
-    halves = []
-    for at in (0, WIDTH):
-        one, two = big[at:at + HALF], big[at + HALF:at + WIDTH]
-        left = one[:, :WIDTH] + swap_halves(two[:, :WIDTH])
-        right = swap_halves(one[:, WIDTH:]) + two[:, WIDTH:]
-        halves.append(jnp.where(low, left, right))
-    return jnp.concatenate(halves, axis=0)
-
-
-def expanded(turn, is_first):
-    low = iota((HALF, WIDTH), 1) < HALF
-    out = []
-    for at in (0, HALF):
-        rows = turn[at:at + HALF]
-        moved = swap_halves(rows)
-        for keep in (low, ~low):
-            to_upper = jnp.where(keep, rows if keep is low else moved, 0.0)
-            to_lower = jnp.where(keep, moved if keep is low else rows, 0.0)
-            one = jnp.where(is_first, to_lower, to_upper)
-            two = jnp.where(is_first, to_upper, to_lower)
-            out.append(jnp.concatenate([one, two], axis=1))
-    return jnp.concatenate(out, axis=0)
-
-
 def loop(low, high, act):
     def body(at, _):
         act(at)
@@ -185,14 +143,14 @@
 
 def kernel(
     slots, x_in, v_in, x_out, v_out,
-    panels, staged, gram_sum, turn_parts, held, moving, edge_out, edge_in, waves, weights,
-    load_sem, store_sem, send_sem, recv_sem, out_send, in_recv,
+    panels, staged, parts_of, gram_sum, turn_parts, start, order, spread, wide,
+    held, moving, edge_out, edge_in, waves, weights,
+    load_sem, store_sem, keep_sem, send_sem, recv_sem, out_send, in_recv,
     edge_send, edge_recv, wave_send, wave_recv, passing, hop_send, hop_recv, pass_send,
 ):
-    packed = panels.shape[1]
     share = held.shape[1]
     bend = share // 2
-    chunks = packed // ROWS
+    chunks, _, length = panels.shape[1:]
     me = lax.axis_index("pair")
     factor = lax.axis_index("factor")
     right = lax.rem(me + 1, slots)
@@ -216,7 +174,7 @@
             device_id=(factor, device), device_id_type=MESH,
         )
 
-    def rows_of(chunk, size=ROWS):
+    def rows_of(chunk, size):
         return pl.ds(pl.multiple_of(chunk * size, size), size)
 
     def place(step, side):
@@ -225,7 +183,7 @@
     def block(step, chunk, side, device):
         at = place(step, side)
         return remote(
-            panels.at[at, rows_of(chunk)], panels.at[at + 2, rows_of(chunk)],
+            panels.at[at, chunk], panels.at[at + 2, chunk],
             send_sem.at[at, chunk], recv_sem.at[at, chunk], device,
         )
 
@@ -321,11 +279,21 @@
         pl.when(jnp.logical_not(last_ring))(act_right)
         pl.when(jnp.logical_not(first_ring))(act_left)
 
-    load = pltpu.make_async_copy(x_in, staged, load_sem.at[0])
-    load.start()
+    def load(chunk):
+        at = rows_of(chunk, length)
+        return pltpu.make_async_copy(x_in.at[at], staged.at[at], load_sem.at[chunk])
+
+    def store(chunk):
+        at = rows_of(chunk, length)
+        return pltpu.make_async_copy(staged.at[at], x_out.at[at], store_sem.at[chunk])
+
     keep_in = pltpu.make_async_copy(
-        v_in.at[rows_of(own, share)], held.at[own], load_sem.at[1]
+        v_in.at[rows_of(own, share)], held.at[own], keep_sem.at[0]
     )
+    keep_out = pltpu.make_async_copy(
+        held.at[own], v_out.at[rows_of(own, share)], keep_sem.at[1]
+    )
+    loop(0, chunks, lambda chunk: load(chunk).start())
     keep_in.start()
 
     barrier = pltpu.get_barrier_semaphore()
@@ -343,42 +311,31 @@
         hop(0, side).start()
     send_piece(0, twin)
 
-    def pack():
-        low = iota((ROWS, WIDTH), 1) < HALF
-
-        def one(chunk):
-            upper, lower = staged[rows_of(chunk)], staged[rows_of(chunk + chunks)]
-            panels[0, rows_of(chunk)] = jnp.where(low, upper, swap_halves(lower))
-            panels[1, rows_of(chunk)] = jnp.where(low, swap_halves(upper), lower)
-
-        loop(0, chunks, one)
-
-    def unpack():
-        low = iota((ROWS, WIDTH), 1) < HALF
-
-        def one(chunk):
-            upper = panels[place(STEPS, 0), rows_of(chunk)]
-            lower = panels[place(STEPS, 1), rows_of(chunk)]
-            staged[rows_of(chunk)] = jnp.where(low, upper, swap_halves(lower))
-            staged[rows_of(chunk + chunks)] = jnp.where(low, swap_halves(upper), lower)
-
-        loop(0, chunks, one)
-
-    def panel_rows(step, at):
-        return jnp.concatenate(
-            [panels[place(step, 0), at], panels[place(step, 1), at]], axis=1
-        )
+    rows = iota((WIDTH, WIDTH), 0)
+    lanes = iota((WIDTH, WIDTH), 1)
+    start[...] = jnp.where(order_of(rows, 0) == lanes, 1.0, 0.0).astype(F32)
+    for swapped in range(2):
+        order[swapped] = final_order(swapped)
+    for line in range(16):
+        picked = lax.rem(iota((2 * WIDTH, WIDTH), 0), 16) == line
+        spread[:, line * WIDTH:(line + 1) * WIDTH] = jnp.where(picked, 1.0, 0.0).astype(BF16)
 
     def gram(step):
         gram_sum[...] = jnp.zeros_like(gram_sum)
-        inner = lambda a, b: lax.dot_general(
-            a, b, (((0,), (0,)), ((), ())), preferred_element_type=F32
-        )
-
-        def add(chunk):
-            @pl.when(step > 0)
-            def _():
-                wait_received(step - 1, chunk)
+
+        def add(chunk, panel):
+            both = jnp.concatenate(split(panel, 2), axis=0)
+            parts_of[chunk] = both
+            gram_sum[...] += lax.dot_general(
+                both, both, (((1,), (1,)), ((), ())), preferred_element_type=F32
+            )
+
+        def first(chunk):
+            load(chunk).wait()
+            add(chunk, staged[rows_of(chunk, length)].T)
+
+        def later(chunk):
+            wait_received(step - 1, chunk)
 
             @pl.when(chunk == chunks - 1)
             def _():
@@ -396,21 +353,26 @@
                     send_piece(0, above_twin)
                     send_piece(0, below_twin)
 
-            high, low = split(panel_rows(step, rows_of(chunk)), 2)
-            gram_sum[0] += inner(high, high) + inner(low, low)
-            gram_sum[1] += inner(high, low)
-
-        loop(0, chunks, add)
-        mixed = gram_sum[1]
-        return folded(gram_sum[0] + (mixed + mixed.T))
+            upper, lower = panels[place(step, 0), chunk], panels[place(step, 1), chunk]
+            add(chunk, jnp.concatenate([upper, lower], axis=0))
+
+        pl.when(step == 0)(lambda: loop(0, chunks, first))
+        pl.when(step > 0)(lambda: loop(0, chunks, later))
+        total = gram_sum[...]
+        left_sum = total[:WIDTH, :WIDTH] + (total[:WIDTH, WIDTH:] + total[WIDTH:, WIDTH:])
+        return left_sum + total[WIDTH:, :WIDTH]
 
     def apply(step, chunk):
-        at = rows_of(chunk)
-        high, low = split(panel_rows(step, at), 2)
-        dot = lambda a, term: jnp.dot(a, turn_parts[term], preferred_element_type=F32)
-        total = dot(high, 0) + (dot(low, 0) + dot(high, 1) + dot(high, 2))
-        panels[place(step, 0) + 3 * is_last, at] = total[:, :WIDTH]
-        panels[place(step, 1) + is_first, at] = total[:, WIDTH:]
+        out = jnp.dot(turn_parts[...], parts_of[chunk], preferred_element_type=F32)
+        out = out[:WIDTH] + (out[WIDTH:2 * WIDTH] + out[2 * WIDTH:])
+        panels[place(step, 0) + 3 * is_last, chunk] = out[:HALF]
+        panels[place(step, 1) + is_first, chunk] = out[HALF:]
+
+    def unpack(chunk):
+        wait_received(STEPS - 1, chunk)
+        upper, lower = panels[place(STEPS, 0), chunk], panels[place(STEPS, 1), chunk]
+        staged[rows_of(chunk, length)] = jnp.concatenate([upper, lower], axis=0).T
+        store(chunk).start()
 
     low_lanes = iota((share, WIDTH), 1) < HALF
     low_bend = iota((bend, WIDTH), 1) < HALF
@@ -427,18 +389,38 @@
         return jnp.where(low_lanes, moving[now, slot], moving[now, slot + 2])
 
     def prepare(step):
+        def arrive(offset):
+            slot = other(offset)
+            wave(step, slot, slot).wait_recv()
+
+        loop(1, RING, arrive)
+        columns = waves[step].reshape(WIDTH, WIDTH).T[:HALF]
+        high, low = split(columns, 2)
+        both = jnp.concatenate([high, low], axis=1)
+        slot_of = lax.rem(iota((HALF, 2 * WIDTH), 1), WIDTH) // 16
+        apart = [jnp.where(slot_of == slot, both, 0).astype(BF16) for slot in range(RING)]
+        wide[...] = jnp.dot(
+            jnp.concatenate(apart, axis=0), spread[...], preferred_element_type=F32
+        )
+
         def one(slot):
-            @pl.when(slot != own)
-            def _():
-                wave(step, slot, slot).wait_recv()
-
-            high, low = multiplied_out(waves[step, slot])
-            first_slot = first_ring & (slot == 0)
-            high = jnp.where(first_slot, swap_halves(high), high)
-            low = jnp.where(first_slot, swap_halves(low), low)
-            weights[step, slot] = jnp.concatenate([high, low], axis=1).astype(BF16)
-
-        loop(0, RING, one)
+            at = rows_of(slot, HALF)
+            turn_a, turn_b = start[:HALF], start[HALF:]
+            for round_no in range(INNER_ROUNDS):
+                line = lambda n: wide[at, n * WIDTH:(n + 1) * WIDTH]
+                cosine, sine = line(round_no), line(INNER_ROUNDS + round_no)
+                turn_a, turn_b = cosine * turn_a + sine * turn_b, cosine * turn_b - sine * turn_a
+                if round_no + 1 < INNER_ROUNDS:
+                    turn_a, turn_b = moved_on(turn_a, turn_b)
+            swapped = (1 - (me + slots - RING) // slots) * (1 - (slot + RING - 1) // RING)
+            turn = jnp.concatenate([turn_a, turn_b], axis=0)
+            weights[step, slot] = jnp.concatenate(in_order(turn, order[swapped], 2), axis=0)
+
+        def two(pair):
+            one(2 * pair)
+            one(2 * pair + 1)
+
+        loop(0, RING // 2, two)
 
     def take_edges(step, now):
         def from_left():
@@ -463,9 +445,10 @@
         def one(slot):
             high, low = split(slot_rows(now, slot), 2)
             weight = weights[step, slot]
-            both = jnp.dot(
+            both = lax.dot_general(
                 jnp.concatenate([high, low], axis=1),
-                jnp.concatenate([weight, weight], axis=0),
+                jnp.concatenate([weight, weight], axis=1),
+                (((1,), (1,)), ((), ())),
                 preferred_element_type=F32,
             )
             moving[later, slot + 1] = both[:, :WIDTH] + both[:, WIDTH:]
@@ -494,13 +477,12 @@
         def _():
             moving[later, RING + 1] = swap_halves(moving[later, RING])
 
-    load.wait()
-    pack()
-
     def one_step(step):
-        turn, own_waves = rotations(gram(step))
-        for term, part in enumerate(split(expanded(turn, is_first == 1), 3)):
-            turn_parts[term] = part
+        turn, own_waves = rotations(gram(step), start[...])
+        parts = in_order(turn, order[is_first], 3)
+        for at, part in enumerate(parts):
+            again = part if at < 2 else jnp.zeros_like(part)
+            turn_parts[at * WIDTH:(at + 1) * WIDTH] = jnp.concatenate([part, again], axis=1)
 
         def turn_columns(chunk):
             apply(step, chunk)
@@ -534,16 +516,8 @@
         gather_rows(peer)
         send_piece(1, peer)
     gather_rows(own)
-    keep_out = pltpu.make_async_copy(
-        held.at[own], v_out.at[rows_of(own, share)], store_sem.at[1]
-    )
     keep_out.start()
-
-    loop(0, chunks, lambda chunk: wait_received(STEPS - 1, chunk))
-    unpack()
-    store = pltpu.make_async_copy(staged, x_out, store_sem.at[0])
-    store.start()
-
+    loop(0, chunks, unpack)
     forward(1)
 
     def settle(step):
@@ -558,14 +532,15 @@
     wait_pieces_sent(0)
     wait_pieces_sent(1)
     wait_pieces(1)
-    store.wait()
+    loop(0, chunks, lambda chunk: store(chunk).wait())
     keep_out.wait()
 
 
 def on_device(columns, basis):
     rows, width = columns.shape
     slots = lax.axis_size("pair")
-    packed = rows // 2
+    length = min(LONG, rows)
+    chunks = rows // length
     share = rows // RING
     shape = jax.ShapeDtypeStruct((rows, width), F32)
     dma = pltpu.SemaphoreType.DMA
@@ -575,20 +550,26 @@
         in_specs=[pl.BlockSpec(memory_space=pl.ANY)] * 2,
         out_specs=(pl.BlockSpec(memory_space=pl.ANY),) * 2,
         scratch_shapes=[
-            pltpu.VMEM((2 * STEPS + 2, packed, width), F32),
+            pltpu.VMEM((2 * STEPS + 2, chunks, width // 2, length), F32),
             pltpu.VMEM((rows, width), F32),
-            pltpu.VMEM((2, 2 * width, 2 * width), F32),
-            pltpu.VMEM((3, 2 * width, 2 * width), BF16),
+            pltpu.VMEM((chunks, 2 * width, length), BF16),
+            pltpu.VMEM((2 * width, 2 * width), F32),
+            pltpu.VMEM((3 * width, 2 * width), BF16),
+            pltpu.VMEM((width, width), F32),
+            pltpu.VMEM((2, width, width), BF16),
+            pltpu.VMEM((2 * width, 16 * width), BF16),
+            pltpu.VMEM((RING * width // 2, 16 * width), F32),
             pltpu.VMEM((RING, share, width), F32),
             pltpu.VMEM((2, RING + 2, share, width), F32),
             pltpu.VMEM((STEPS, 2, share // 2, width), F32),
             pltpu.VMEM((STEPS, 2, share // 2, width), F32),
             pltpu.VMEM((STEPS, RING, 16, width), F32),
-            pltpu.VMEM((STEPS, RING, width, 2 * width), BF16),
+            pltpu.VMEM((STEPS, RING, 2 * width, width), BF16),
+            dma((chunks,)),
+            dma((chunks,)),
             dma((2,)),
-            dma((2,)),
-            dma((2 * STEPS, packed // ROWS)),
-            dma((2 * STEPS, packed // ROWS)),
+            dma((2 * STEPS, chunks)),
+            dma((2 * STEPS, chunks)),
             dma((2, RING)),
             dma((2, RING)),
             dma((STEPS, 2)),

time: 172 us -> 169 us (0.983)
  Pallas kernels: 168 us -> 165 us
    pallas_call x1, Pallas kernels: 168 us -> 165 us  [on_device(): pl.pallas_call(functools.partial(kernel, slots), out_shape=(shape, shape)...]
where the time goes in v4:
time: 169 us
  Pallas kernels  165 us (98%)
  local copies, waits for them, and re-layouts  3.66 us (2%)
    pallas_call x1, Pallas kernels, on_device(): pl.pallas_call(functools.partial(kernel, slots), out_shape=(shape, shape)...  165 us
    unnamed x4, local copies, waits for them, and re-layouts  3.66 us

profile of v4, /device:TPU:1, one launch (start us, length us, event | category | flops | bytes accessed | tf_op | source)
XLA Modules:
  0.0 169.0 jit_solution(11097757954374903918)
XLA Ops:
  0.6 164.7 %shard_map.41 = (f32[4096,128]{1,0:T(8,128)S(1)}, f32[4096,128]{1,0:T(8,128)}) custom-call(f32[4096,128]{1,0:T(8,128)} %x_in.1, f32[4096,128]{1,0:T(8,128)} %v_in.1), custom_call_target="tpu_custom_call" | custom-call | flops 7247757312 | bytes 8388608 | tf_op jit(solution)/shard_map/pallas_call | solution.py:547
  165.4 0.0 copy-start
  165.4 1.3 copy.6
  166.7 1.0 copy-done
  167.7 1.3 copy.7
Async XLA Ops:
  165.4 2.3 %copy-start = (f32[4096,128]{1,0:T(8,128)S(1)}, f32[4096,128]{1,0:T(8,128)}, u32[]{:S(2)}) copy-start(f32[4096,128]{1,0:T(8,128)} %get-tuple-element.5) | copy-start | bytes 6291460

commit v5 on v1

v5 whole, which is shorter than its diff:
```python
import functools

import jax
import jax.numpy as jnp
from jax import lax
from jax.experimental import pallas as pl
from jax.experimental.pallas import tpu as pltpu
from jax.sharding import PartitionSpec as P

STEPS = 6
INNER_ROUNDS = 8
MESH = pl.DeviceIdType.MESH
F32 = jnp.float32
BF16 = jnp.bfloat16
WIDTH = 128
HALF = 64
LONG = 1024


def iota(shape, dim):
    return lax.broadcasted_iota(jnp.int32, shape, dim)


def sublane_roll(value, shift):
    return pltpu.roll(value, shift % 8, 0)


def order_of(row, shift):
    inside = lax.rem(row, HALF)
    k = 8 * lax.rem(inside, 8) + inside // 8
    k = jnp.where(row < HALF, k, WIDTH - 1 - k)
    return jnp.where(k == 0, 0, 1 + lax.rem(k - 1 + shift, WIDTH - 1))


def moved_on(first, second):
    top = iota((8, first.shape[1]), 0) == 0
    end = iota((8, first.shape[1]), 0) == 7
    a, b = first, second
    new_first = jnp.concatenate(
        [
            jnp.where(top, a[:8], a[8:16]),
            a[16:],
            jnp.where(end, b[HALF - 8:], sublane_roll(a[:8], -1)),
        ],
        axis=0,
    )
    new_second = jnp.concatenate(
        [jnp.where(top, a[8:16], sublane_roll(b[HALF - 8:], 1)), b[:HALF - 8]], axis=0
    )
    return new_first, new_second


def angles(diag_a, diag_b, cross):
    spread = diag_a - diag_b
    twice = 2.0 * cross
    twice = jnp.where(spread >= 0.0, twice, -twice)
    size = jnp.abs(spread)
    most = jnp.maximum(size, jnp.abs(twice))
    still = most == 0.0
    scale = pl.reciprocal(jnp.where(still, 1.0, most), approx=True)
    size = jnp.where(still, 1.0, size * scale)
    twice = twice * scale
    inverse = lax.rsqrt(size * size + twice * twice)
    cos_sq = 0.5 + 0.5 * size * inverse
    inverse_cos = lax.rsqrt(cos_sq)
    return cos_sq * inverse_cos, 0.5 * twice * inverse * inverse_cos


def lane_sum(value):
    return jnp.broadcast_to(jnp.sum(value, axis=1, keepdims=True), value.shape)


def rotations(gram, start):
    order = start.astype(BF16)
    pieces = [jnp.dot(order, part, preferred_element_type=F32) for part in split(gram, 3)]
    ordered = (pieces[0] + pieces[1]) + pieces[2]
    turn_a, turn_b = start[:HALF], start[HALF:]
    with_a, with_b = ordered[:HALF], ordered[HALF:]
    diag_a, diag_b = lane_sum(turn_a * with_a), lane_sum(turn_b * with_b)
    for round_no in range(INNER_ROUNDS):
        cross = lane_sum(turn_a * with_b)
        cosine, sine = angles(diag_a, diag_b, cross)
        turn_a, turn_b = cosine * turn_a + sine * turn_b, cosine * turn_b - sine * turn_a
        if round_no + 1 < INNER_ROUNDS:
            with_a, with_b = cosine * with_a + sine * with_b, cosine * with_b - sine * with_a
            both = 2.0 * cosine * sine * cross
            cos_sq, sin_sq = cosine * cosine, sine * sine
            diag_a, diag_b = (
                cos_sq * diag_a + sin_sq * diag_b + both,
                cos_sq * diag_b + sin_sq * diag_a - both,
            )
            turn_a, turn_b = moved_on(turn_a, turn_b)
            with_a, with_b = moved_on(with_a, with_b)
            diag_a, diag_b = moved_on(diag_a, diag_b)
    return jnp.concatenate([turn_a, turn_b], axis=0)


def final_order(swapped):
    rows = iota((WIDTH, WIDTH), 0)
    rows = lax.rem(rows + HALF, WIDTH) if swapped else rows
    lanes = iota((WIDTH, WIDTH), 1)
    return jnp.where(order_of(lanes, INNER_ROUNDS - 1) == rows, 1.0, 0.0).astype(BF16)


def in_order(turn, order, parts):
    return [
        jnp.dot(order, part, preferred_element_type=F32).astype(BF16)
        for part in split(turn, parts)
    ]


def swap_halves(value):
    return pltpu.roll(value, HALF, 1)


def split(value, parts):
    out = []
    for _ in range(parts - 1):
        part = value.astype(BF16)
        out.append(part)
        value = value - part.astype(F32)
    out.append(value.astype(BF16))
    return out


def loop(low, high, act):
    def body(at, _):
        act(at)
        return 0

    lax.fori_loop(low, high, body, 0)


def kernel(
    slots, x_in, v_in, x_out, v_out,
    panels, staged, parts_of, gram_sum, turn_parts, start, order,
    load_sem, send_sem, recv_sem,
):
    chunks, _, length = panels.shape[2:]
    me = lax.axis_index("pair")
    factor = lax.axis_index("factor")
    right = lax.rem(me + 1, slots)
    left = lax.rem(me + slots - 1, slots)
    is_first = 1 - (me + slots - 1) // slots
    is_last = (me + 1) // slots

    def rows_of(chunk):
        return pl.ds(pl.multiple_of(chunk * length, length), length)

    def place(step, side):
        return 2 * step + side

    def load(which, chunk):
        return pltpu.make_async_copy(
            (x_in, v_in)[which].at[rows_of(chunk)], staged.at[which, rows_of(chunk)],
            load_sem.at[which, chunk],
        )

    def block(which, step, chunk, side, device):
        at = place(step, side)
        return pltpu.make_async_remote_copy(
            src_ref=panels.at[which, at, chunk],
            dst_ref=panels.at[which, at + 2, chunk],
            send_sem=send_sem.at[which, at, chunk],
            recv_sem=recv_sem.at[which, at, chunk],
            device_id=(factor, device),
            device_id_type=MESH,
        )

    def send_block(which, step, chunk):
        @pl.when(me < slots - 1)
        def _():
            block(which, step, chunk, 0, right).start()

        @pl.when(me > 0)
        def _():
            block(which, step, chunk, 1, left).start()

    def wait_sent(which, step, chunk):
        @pl.when(me < slots - 1)
        def _():
            block(which, step, chunk, 0, right).wait_send()

        @pl.when(me > 0)
        def _():
            block(which, step, chunk, 1, left).wait_send()

    def wait_received(which, step, chunk):
        @pl.when(me > 0)
        def _():
            block(which, step, chunk, 0, right).wait_recv()

        @pl.when(me < slots - 1)
        def _():
            block(which, step, chunk, 1, left).wait_recv()

    for which in range(2):
        loop(0, chunks, lambda chunk: load(which, chunk).start())

    barrier = pltpu.get_barrier_semaphore()
    for neighbour in (left, right):
        pl.semaphore_signal(
            barrier, inc=1, device_id=(factor, neighbour), device_id_type=MESH
        )

    rows = iota((WIDTH, WIDTH), 0)
    lanes = iota((WIDTH, WIDTH), 1)
    start[...] = jnp.where(order_of(rows, 0) == lanes, 1.0, 0.0).astype(F32)
    for swapped in range(2):
        order[swapped] = final_order(swapped)

    def panel(which, step, chunk):
        return jnp.concatenate(
            [panels[which, place(step, 0), chunk], panels[which, place(step, 1), chunk]],
            axis=0,
        )

    def loaded(which, chunk):
        load(which, chunk).wait()
        return staged[which, rows_of(chunk)].T

    def gram(step):
        gram_sum[...] = jnp.zeros_like(gram_sum)

        def add(chunk, value):
            both = jnp.concatenate(split(value, 2), axis=0)
            parts_of[chunk] = both
            gram_sum[...] += lax.dot_general(
                both, both, (((1,), (1,)), ((), ())), preferred_element_type=F32
            )

        def later(chunk):
            wait_received(0, step - 1, chunk)
            add(chunk, panel(0, step, chunk))

        @pl.when(step == 0)
        def _():
            loop(0, chunks, lambda chunk: add(chunk, loaded(0, chunk)))

        pl.when(step > 0)(lambda: loop(0, chunks, later))
        total = gram_sum[...]
        left_sum = total[:WIDTH, :WIDTH] + (total[:WIDTH, WIDTH:] + total[WIDTH:, WIDTH:])
        return left_sum + total[WIDTH:, :WIDTH]

    def give(which, step, chunk, out):
        panels[which, place(step, 0) + 3 * is_last, chunk] = out[:HALF]
        panels[which, place(step, 1) + is_first, chunk] = out[HALF:]
        send_block(which, step, chunk)

    def one_step(step):
        turn = rotations(gram(step), start[...])
        parts = in_order(turn, order[is_first], 3)
        for at, part in enumerate(parts):
            again = part if at < 2 else jnp.zeros_like(part)
            turn_parts[at * WIDTH:(at + 1) * WIDTH] = jnp.concatenate([part, again], axis=1)

        pl.when(step == 0)(lambda: pl.semaphore_wait(barrier, 2))

        def turn_columns(chunk):
            out = jnp.dot(turn_parts[...], parts_of[chunk], preferred_element_type=F32)
            out = out[:WIDTH] + (out[WIDTH:2 * WIDTH] + out[2 * WIDTH:])
            give(0, step, chunk, out)

        loop(0, chunks, turn_columns)

        def turn_basis(chunk, value):
            both = jnp.concatenate(split(value, 2), axis=0)
            out = jnp.dot(turn_parts[:2 * WIDTH], both, preferred_element_type=F32)
            give(1, step, chunk, out[:WIDTH] + out[WIDTH:])

        def later(chunk):
            wait_received(1, step - 1, chunk)
            turn_basis(chunk, panel(1, step, chunk))

        @pl.when(step == 0)
        def _():
            loop(0, chunks, lambda chunk: turn_basis(chunk, loaded(1, chunk)))

        pl.when(step > 0)(lambda: loop(0, chunks, later))

    loop(0, STEPS, one_step)

    for which, target in enumerate((x_out, v_out)):
        def finish(chunk):
            wait_received(which, STEPS - 1, chunk)
            target[rows_of(chunk)] = panel(which, STEPS, chunk).T

        loop(0, chunks, finish)

    def settle(step):
        for which in range(2):
            loop(0, chunks, lambda chunk: wait_sent(which, step, chunk))

    loop(0, STEPS, settle)


def write_out(x, v, x_out, v_out, sem):
    copies = [
        pltpu.make_async_copy(source, target, sem.at[at])
        for at, (source, target) in enumerate(((x, x_out), (v, v_out)))
    ]
    for copy in copies:
        copy.start()
    for copy in copies:
        copy.wait()


def on_device(columns, basis):
    rows, width = columns.shape
    slots = lax.axis_size("pair")
    length = min(LONG, rows)
    chunks = rows // length
    shape = jax.ShapeDtypeStruct((rows, width), F32)
    in_vmem = pltpu.VMEM((rows, width), F32)
    dma = pltpu.SemaphoreType.DMA
    out = pl.pallas_call(
        functools.partial(kernel, slots),
        out_shape=(in_vmem, in_vmem),
        in_specs=[pl.BlockSpec(memory_space=pl.ANY)] * 2,
        out_specs=(pl.BlockSpec(memory_space=pltpu.VMEM),) * 2,
        scratch_shapes=[
            pltpu.VMEM((2, 2 * STEPS + 2, chunks, width // 2, length), F32),
            pltpu.VMEM((2, rows, width), F32),
            pltpu.VMEM((chunks, 2 * width, length), BF16),
            pltpu.VMEM((2 * width, 2 * width), F32),
            pltpu.VMEM((3 * width, 2 * width), BF16),
            pltpu.VMEM((width, width), F32),
            pltpu.VMEM((2, width, width), BF16),
            dma((2, chunks)),
            dma((2, 2 * STEPS, chunks)),
            dma((2, 2 * STEPS, chunks)),
        ],
        compiler_params=pltpu.CompilerParams(
            collective_id=0, has_side_effects=True, vmem_limit_bytes=59 * 2**20
        ),
        cost_estimate=pl.CostEstimate(
            flops=6 * 9 * 2 * rows * width * width,
            bytes_accessed=4 * rows * width * 4,
            transcendentals=0,
        ),
    )(columns, basis)
    return pl.pallas_call(
        write_out,
        out_shape=(shape, shape),
        in_specs=[pl.BlockSpec(memory_space=pltpu.VMEM)] * 2,
        out_specs=(pl.BlockSpec(memory_space=pl.ANY),) * 2,
        scratch_shapes=[dma((2,))],
    )(*out)


def solution(mesh):
    spec = P("factor", "pair")
    return jax.shard_map(
        on_device, mesh=mesh, in_specs=(spec, spec), out_specs=(spec, spec), check_vma=False
    )
```

time: 154 us -> 153 us (level)
    pallas_call x1 -> x2, Pallas kernels: 149 us -> 150 us  [the longest x1 146 us: on_device(): pl.pallas_call(functools.partial(kernel, slots), out_shape=(in_vmem, in_v...]
where the time goes in v5:
time: 153 us
  Pallas kernels  150 us (98%)
  local copies, waits for them, and re-layouts  2.64 us (2%)
    pallas_call x1, Pallas kernels, on_device(): pl.pallas_call(functools.partial(kernel, slots), out_shape=(in_vmem, in_v...  146 us
    pallas_call x1, Pallas kernels, on_device(): pl.pallas_call(write_out, out_shape=(shape, shape), in_specs=[pl.BlockSpe...  4.25 us

profile of v5, /device:TPU:1, one launch (start us, length us, event | category | flops | bytes accessed | tf_op | source)
XLA Modules:
  0.0 153.3 jit_solution(15406328535211512120)
XLA Ops:
  0.6 145.8 %shard_map.41 = (f32[4096,128]{1,0:T(8,128)S(1)}, f32[4096,128]{1,0:T(8,128)S(1)}) custom-call(f32[4096,128]{1,0:T(8,128)} %x_in.1, f32[4096,128]{1,0:T(8,128)} %v_in.1), custom_call_target="tpu_custom_call" | custom-call | flops 7247757312 | bytes 8388608 | tf_op jit(solution)/shard_map/pallas_call | solution.py:316
  146.4 0.0 copy-start
  146.5 1.3 copy-done
  147.8 0.0 copy-start.1
  147.8 1.3 copy-done.1
  149.1 4.2 %shard_map.42 = (f32[4096,128]{1,0:T(8,128)}, f32[4096,128]{1,0:T(8,128)}) custom-call(f32[4096,128]{1,0:T(8,128)} %copy-done, f32[4096,128]{1,0:T(8,128)} %copy-done.1), custom_call_target="tpu_custom_call" | custom-call | tf_op jit(solution)/shard_map/pallas_call | solution.py:342
Async XLA Ops:
  146.4 1.3 copy-start
  147.8 1.3 copy-start.1

commit v6 on v5

--- a/solution.py
+++ b/solution.py
@@ -342,9 +342,10 @@
     return pl.pallas_call(
         write_out,
         out_shape=(shape, shape),
-        in_specs=[pl.BlockSpec(memory_space=pltpu.VMEM)] * 2,
+        in_specs=[pl.BlockSpec(memory_space=pl.ANY)] * 2,
         out_specs=(pl.BlockSpec(memory_space=pl.ANY),) * 2,
         scratch_shapes=[dma((2,))],
+        compiler_params=pltpu.CompilerParams(vmem_limit_bytes=2**20),
     )(*out)
 
 

time: 153 us -> 149 us (0.974)
  local copies, waits for them, and re-layouts: 2.64 us -> 0 us
  Pallas kernels: 150 us -> 148 us
    unnamed x4 -> x0, local copies, waits for them, and re-layouts: 2.64 us -> none
    pallas_call x1, Pallas kernels: 4.25 us -> 2.03 us  [on_device(): pl.pallas_call(write_out, out_shape=(shape, shape), in_specs=[pl.BlockSpe...]
where the time goes in v6:
time: 149 us; the launch traced here: 148 us
  Pallas kernels  148 us (99%)
    pallas_call x1, Pallas kernels, on_device(): pl.pallas_call(functools.partial(kernel, slots), out_shape=(in_vmem, in_v...  146 us

profile of v6, /device:TPU:1, one launch (start us, length us, event | category | flops | bytes accessed | tf_op | source)
XLA Modules:
  0.0 148.5 jit_solution(46099419642741191)
XLA Ops:
  0.6 145.8 %shard_map.41 = (f32[4096,128]{1,0:T(8,128)S(1)}, f32[4096,128]{1,0:T(8,128)S(1)}) custom-call(f32[4096,128]{1,0:T(8,128)} %x_in.1, f32[4096,128]{1,0:T(8,128)} %v_in.1), custom_call_target="tpu_custom_call" | custom-call | flops 7247757312 | bytes 8388608 | tf_op jit(solution)/shard_map/pallas_call | solution.py:316
  146.4 2.0 %shard_map.42 = (f32[4096,128]{1,0:T(8,128)}, f32[4096,128]{1,0:T(8,128)}) custom-call(f32[4096,128]{1,0:T(8,128)S(1)} %get-tuple-element.4.x, f32[4096,128]{1,0:T(8,128)S(1)} %get-tuple-element.5.v), custom_call_target="tpu_custom_call" | custom-call | tf_op jit(solution)/shard_map/pallas_call | solution.py:342

commit v7 on v6

--- a/solution.py
+++ b/solution.py
@@ -133,8 +133,8 @@
 
 def kernel(
     slots, x_in, v_in, x_out, v_out,
-    panels, staged, parts_of, gram_sum, turn_parts, start, order,
-    load_sem, send_sem, recv_sem,
+    panels, staged, parts_of, gram_sum, turn_parts, start, order, raw, turn_give, turn_take,
+    load_sem, send_sem, recv_sem, raw_send, raw_recv, turn_send, turn_recv,
 ):
     chunks, _, length = panels.shape[2:]
     me = lax.axis_index("pair")
@@ -167,6 +167,27 @@
             device_id_type=MESH,
         )
 
+    def remote(src, dst, send, recv, device):
+        return pltpu.make_async_remote_copy(
+            src_ref=src, dst_ref=dst, send_sem=send, recv_sem=recv,
+            device_id=(factor, device), device_id_type=MESH,
+        )
+
+    def as_came(side):
+        return remote(
+            v_in.at[rows_of(0)], raw.at[side], raw_send.at[side], raw_recv.at[side],
+            (right, left)[side],
+        )
+
+    def turn_rows(side):
+        return remote(
+            turn_give.at[side], turn_take.at[side], turn_send.at[side], turn_recv.at[side],
+            (right, left)[side],
+        )
+
+    gives = (me < slots - 1, me > 0)
+    takes = (me > 0, me < slots - 1)
+
     def send_block(which, step, chunk):
         @pl.when(me < slots - 1)
         def _():
@@ -202,6 +223,9 @@
         pl.semaphore_signal(
             barrier, inc=1, device_id=(factor, neighbour), device_id_type=MESH
         )
+    pl.semaphore_wait(barrier, 2)
+    for side in range(2):
+        pl.when(gives[side])(lambda: as_came(side).start())
 
     rows = iota((WIDTH, WIDTH), 0)
     lanes = iota((WIDTH, WIDTH), 1)
@@ -247,6 +271,25 @@
         panels[which, place(step, 1) + is_first, chunk] = out[HALF:]
         send_block(which, step, chunk)
 
+    def turn_neighbour(side):
+        @pl.when(takes[side])
+        def _():
+            as_came(side).wait_recv()
+            turn_rows(side).wait_recv()
+
+        @pl.when(jnp.logical_not(takes[side]))
+        def _():
+            raw[side] = staged[1, rows_of(0)]
+            turn_take[side] = turn_give[1 - side]
+
+        high, low = split(turn_take[side], 2)
+        lhs = jnp.concatenate([high, low], axis=0)
+        both = jnp.concatenate(split(raw[side].T, 2), axis=0)
+        out = jnp.dot(
+            jnp.concatenate([lhs, lhs], axis=1), both, preferred_element_type=F32
+        )
+        panels[1, place(1, side), 0] = out[:HALF] + out[HALF:]
+
     def one_step(step):
         turn = rotations(gram(step), start[...])
         parts = in_order(turn, order[is_first], 3)
@@ -254,8 +297,6 @@
             again = part if at < 2 else jnp.zeros_like(part)
             turn_parts[at * WIDTH:(at + 1) * WIDTH] = jnp.concatenate([part, again], axis=1)
 
-        pl.when(step == 0)(lambda: pl.semaphore_wait(barrier, 2))
-
         def turn_columns(chunk):
             out = jnp.dot(turn_parts[...], parts_of[chunk], preferred_element_type=F32)
             out = out[:WIDTH] + (out[WIDTH:2 * WIDTH] + out[2 * WIDTH:])
@@ -269,12 +310,22 @@
             give(1, step, chunk, out[:WIDTH] + out[WIDTH:])
 
         def later(chunk):
-            wait_received(1, step - 1, chunk)
+            pl.when((step > 1) | (chunk > 0))(lambda: wait_received(1, step - 1, chunk))
             turn_basis(chunk, panel(1, step, chunk))
 
         @pl.when(step == 0)
         def _():
-            loop(0, chunks, lambda chunk: turn_basis(chunk, loaded(1, chunk)))
+            for side in range(2):
+                high, low = (
+                    turn_parts[at:at + HALF, :WIDTH].astype(F32)
+                    for at in (side * HALF, WIDTH + side * HALF)
+                )
+                turn_give[side] = high + low
+                pl.when(gives[side])(lambda: turn_rows(side).start())
+            loop(1, chunks, lambda chunk: turn_basis(chunk, loaded(1, chunk)))
+            load(1, 0).wait()
+            for side in range(2):
+                turn_neighbour(side)
 
         pl.when(step > 0)(lambda: loop(0, chunks, later))
 
@@ -288,17 +339,25 @@
         loop(0, chunks, finish)
 
     def settle(step):
-        for which in range(2):
-            loop(0, chunks, lambda chunk: wait_sent(which, step, chunk))
+        loop(0, chunks, lambda chunk: wait_sent(0, step, chunk))
+        none = 1 - (step + STEPS - 1) // STEPS
+        loop(none, chunks, lambda chunk: wait_sent(1, step, chunk))
 
     loop(0, STEPS, settle)
+    for side in range(2):
+        pl.when(gives[side])(lambda: as_came(side).wait_send())
+        pl.when(gives[side])(lambda: turn_rows(side).wait_send())
 
 
 def write_out(x, v, x_out, v_out, sem):
-    copies = [
-        pltpu.make_async_copy(source, target, sem.at[at])
-        for at, (source, target) in enumerate(((x, x_out), (v, v_out)))
-    ]
+    length = x.shape[0] // sem.shape[1]
+    copies = []
+    for chunk in range(sem.shape[1]):
+        at = pl.ds(chunk * length, length)
+        for which, (source, target) in enumerate(((x, x_out), (v, v_out))):
+            copies.append(
+                pltpu.make_async_copy(source.at[at], target.at[at], sem.at[which, chunk])
+            )
     for copy in copies:
         copy.start()
     for copy in copies:
@@ -326,9 +385,16 @@
             pltpu.VMEM((3 * width, 2 * width), BF16),
             pltpu.VMEM((width, width), F32),
             pltpu.VMEM((2, width, width), BF16),
+            pltpu.VMEM((2, length, width), F32),
+            pltpu.VMEM((2, width // 2, width), F32),
+            pltpu.VMEM((2, width // 2, width), F32),
             dma((2, chunks)),
             dma((2, 2 * STEPS, chunks)),
             dma((2, 2 * STEPS, chunks)),
+            dma((2,)),
+            dma((2,)),
+            dma((2,)),
+            dma((2,)),
         ],
         compiler_params=pltpu.CompilerParams(
             collective_id=0, has_side_effects=True, vmem_limit_bytes=59 * 2**20
@@ -344,7 +410,7 @@
         out_shape=(shape, shape),
         in_specs=[pl.BlockSpec(memory_space=pl.ANY)] * 2,
         out_specs=(pl.BlockSpec(memory_space=pl.ANY),) * 2,
-        scratch_shapes=[dma((2,))],
+        scratch_shapes=[dma((2, 4))],
         compiler_params=pltpu.CompilerParams(vmem_limit_bytes=2**20),
     )(*out)
 

time: 149 us -> 149 us (level)
  no operation moved by 1% of the time
where the time goes in v7:
time: 149 us; the launch traced here: 148 us
  Pallas kernels  147 us (99%)
    pallas_call x1, Pallas kernels, on_device(): pl.pallas_call(functools.partial(kernel, slots), out_shape=(in_vmem, in_v...  145 us

profile of v7, /device:TPU:1, one launch (start us, length us, event | category | flops | bytes accessed | tf_op | source)
XLA Modules:
  0.0 147.5 jit_solution(12172086023282895128)
XLA Ops:
  0.6 144.8 %shard_map.41 = (f32[4096,128]{1,0:T(8,128)S(1)}, f32[4096,128]{1,0:T(8,128)S(1)}) custom-call(f32[4096,128]{1,0:T(8,128)} %x_in.1, f32[4096,128]{1,0:T(8,128)} %v_in.1), custom_call_target="tpu_custom_call" | custom-call | flops 7247757312 | bytes 8388608 | tf_op jit(solution)/shard_map/pallas_call | solution.py:375
  145.5 2.1 %shard_map.42 = (f32[4096,128]{1,0:T(8,128)}, f32[4096,128]{1,0:T(8,128)}) custom-call(f32[4096,128]{1,0:T(8,128)S(1)} %get-tuple-element.4.x, f32[4096,128]{1,0:T(8,128)S(1)} %get-tuple-element.5.v), custom_call_target="tpu_custom_call" | custom-call | tf_op jit(solution)/shard_map/pallas_call | solution.py:408

commit v8 on v7

--- a/solution.py
+++ b/solution.py
@@ -323,6 +323,9 @@
                 turn_give[side] = high + low
                 pl.when(gives[side])(lambda: turn_rows(side).start())
             loop(1, chunks, lambda chunk: turn_basis(chunk, loaded(1, chunk)))
+
+        @pl.when(step == 1)
+        def _():
             load(1, 0).wait()
             for side in range(2):
                 turn_neighbour(side)

time: 149 us -> 149 us (level)
  no operation moved by 1% of the time
where the time goes in v8:
time: 149 us; the launch traced here: 148 us
  Pallas kernels  147 us (99%)
    pallas_call x1, Pallas kernels, on_device(): pl.pallas_call(functools.partial(kernel, slots), out_shape=(in_vmem, in_v...  145 us

profile of v8, /device:TPU:1, one launch (start us, length us, event | category | flops | bytes accessed | tf_op | source)
XLA Modules:
  0.0 147.5 jit_solution(10709599076022747464)
XLA Ops:
  0.6 144.8 %shard_map.41 = (f32[4096,128]{1,0:T(8,128)S(1)}, f32[4096,128]{1,0:T(8,128)S(1)}) custom-call(f32[4096,128]{1,0:T(8,128)} %x_in.1, f32[4096,128]{1,0:T(8,128)} %v_in.1), custom_call_target="tpu_custom_call" | custom-call | flops 7247757312 | bytes 8388608 | tf_op jit(solution)/shard_map/pallas_call | solution.py:378
  145.5 2.1 %shard_map.42 = (f32[4096,128]{1,0:T(8,128)}, f32[4096,128]{1,0:T(8,128)}) custom-call(f32[4096,128]{1,0:T(8,128)S(1)} %get-tuple-element.4.x, f32[4096,128]{1,0:T(8,128)S(1)} %get-tuple-element.5.v), custom_call_target="tpu_custom_call" | custom-call | tf_op jit(solution)/shard_map/pallas_call | solution.py:411
